TPU v7x, 256 devices: a whole 4x4x8 slice. The times are simulated.
256 devices in a mesh: pts: 256 (over x, y, z, core).
Axes of the slice: x: 4, y: 4, z: 8, core: 2. Of those that a mesh axis runs over, the one named last changes fastest.
Arguments:
- points: bfloat16 [262144, 256], P('pts'), may hold values from -6 to 6
- cotangent: bfloat16 [262144, 256], P('pts'), may hold values from -6 to 6
- ln1_gain: float32 [256], replicated, may hold values from 0.5 to 1.5
- w_x: bfloat16 [256, 256], replicated, may hold values from -0.375 to 0.375
- w_fx: bfloat16 [256, 256], replicated, may hold values from -0.375 to 0.375
- w_slice: float32 [32, 64], replicated, may hold values from -1 to 1
- temp_base: float32 [8], replicated, may hold values from 0.5 to 2
- ada_vec: float32 [32], replicated, may hold values from -1 to 1
- query_matrix: float32 [32, 32], replicated, may hold values from -1 to 1
- key_matrix: float32 [32, 32], replicated, may hold values from -1 to 1
- value_matrix: float32 [32, 32], replicated, may hold values from -1 to 1
- w_out: bfloat16 [256, 256], replicated, may hold values from -0.375 to 0.375
- ln2_gain: float32 [256], replicated, may hold values from 0.5 to 1.5
- w_up: bfloat16 [256, 1024], replicated, may hold values from -0.375 to 0.375
- b_up: float32 [1024], replicated, may hold values from -3 to 3
- w_down: bfloat16 [1024, 256], replicated, may hold values from -0.1875 to 0.1875
Outputs:
- grad_points: bfloat16 [262144, 256], P('pts')
- g_gain1: float32 [256], replicated
- g_x: float32 [256, 256], replicated
- g_fx: float32 [256, 256], replicated
- g_slice: float32 [32, 64], replicated
- g_base: float32 [8], replicated
- g_ada: float32 [32], replicated
- g_q: float32 [32, 32], replicated
- g_k: float32 [32, 32], replicated
- g_v: float32 [32, 32], replicated
- g_out: float32 [256, 256], replicated
- g_gain2: float32 [256], replicated
- g_up: float32 [256, 1024], replicated
- g_bup: float32 [1024], replicated
- g_down: float32 [1024, 256], replicated
All inputs are finite; a program needn't handle non-finite values.
Results may differ from a plain program's by a relative error of at most 0.0066.
Values sent between devices are 32-bit elements; how exact they have to be, the bound alone decides.
A program may use at most 64 MiB of HBM per device.

v0:
```python
import jax
import jax.numpy as jnp
from jax import lax
from jax.sharding import PartitionSpec as P

HIGH_INDEX = lax.Precision.HIGHEST


def layer_norm(value_rows, gain):
    centered = value_rows - jnp.mean(value_rows, axis=-1, keepdims=True)
    spread = jnp.mean(centered * centered, axis=-1, keepdims=True)
    return centered * lax.rsqrt(spread + 1e-05) * gain


def slice_weights(mid, w_slice, temp_base, ada_vec):
    point_count = mid.shape[0]
    split = mid.reshape(point_count, temp_base.shape[0], -1)
    tilt = jnp.tanh(jnp.einsum("phd,d->ph", split, ada_vec, precision=HIGH_INDEX))
    temper = temp_base[None, :] * jnp.exp(0.5 * tilt)
    logits = jnp.einsum("phd,dm->phm", split, w_slice, precision=HIGH_INDEX) / temper[:, :, None]
    raised = jnp.exp(logits)
    return raised / jnp.sum(raised, axis=-1, keepdims=True)


def front(points, ln1_gain, w_x, w_fx, w_slice, temp_base, ada_vec):
    normed, ln_back = jax.vjp(layer_norm, points.astype(jnp.float32), ln1_gain)
    normed_b = normed.astype(jnp.bfloat16)
    mid = jnp.dot(normed_b, w_x, preferred_element_type=jnp.float32)
    feat = jnp.dot(normed_b, w_fx, preferred_element_type=jnp.float32)
    slice_weight_rows, weight_back = jax.vjp(slice_weights, mid, w_slice, temp_base, ada_vec)
    feature_head_rows = feat.reshape(slice_weight_rows.shape[0], slice_weight_rows.shape[1], -1)
    numerator_total = jnp.einsum(
        "skn,ske->kne", slice_weight_rows, feature_head_rows, precision=HIGH_INDEX
    )
    denom = jnp.sum(slice_weight_rows, axis=0)
    return (
        normed_b,
        ln_back,
        weight_back,
        slice_weight_rows,
        feature_head_rows,
        numerator_total,
        denom,
    )


def tokens_out(numerator_total, denom, query_matrix, key_matrix, value_matrix):
    token_rows = numerator_total / (denom[:, :, None] + 1e-05)
    query_rows = jnp.einsum("lct,ty->lcy", token_rows, query_matrix, precision=HIGH_INDEX)
    key_rows = jnp.einsum("lct,ty->lcy", token_rows, key_matrix, precision=HIGH_INDEX)
    value_rows = jnp.einsum("lct,ty->lcy", token_rows, value_matrix, precision=HIGH_INDEX)
    scores = jnp.einsum(
        "hme,hne->hmn", query_rows, key_rows, precision=HIGH_INDEX
    ) * query_matrix.shape[0] ** (-0.5)
    raised = jnp.exp(scores)
    attn = raised / jnp.sum(raised, axis=-1, keepdims=True)
    return jnp.einsum("hmn,hne->hme", attn, value_rows, precision=HIGH_INDEX)


def back_top(
    points, cotangent, slice_weight_rows, slice_output, ln2_gain, w_out, w_up, b_up, w_down
):
    point_count = slice_weight_rows.shape[0]
    heads = slice_weight_rows.shape[1]
    blended_tokens = jnp.einsum(
        "iwe,web->iwb", slice_weight_rows, slice_output, precision=HIGH_INDEX
    ).reshape(point_count, -1)
    mixed_b = blended_tokens.astype(jnp.bfloat16)
    first = points.astype(jnp.float32) + jnp.dot(mixed_b, w_out, preferred_element_type=jnp.float32)
    normed, ln_back = jax.vjp(layer_norm, first, ln2_gain)
    normed_b = normed.astype(jnp.bfloat16)
    pre = jnp.dot(normed_b, w_up, preferred_element_type=jnp.float32) + b_up
    act, gelu_back = jax.vjp(jax.nn.gelu, pre)
    act_b = act.astype(jnp.bfloat16)
    g_down = jnp.einsum("pf,pc->fc", act_b, cotangent, preferred_element_type=jnp.float32)
    d_act = jnp.einsum("pc,fc->pf", cotangent, w_down, preferred_element_type=jnp.float32)
    d_pre = gelu_back(d_act)[0]
    g_bup = jnp.sum(d_pre, axis=0)
    d_pre_b = d_pre.astype(jnp.bfloat16)
    g_up = jnp.einsum("pc,pf->cf", normed_b, d_pre_b, preferred_element_type=jnp.float32)
    d_normed = jnp.einsum("pf,cf->pc", d_pre_b, w_up, preferred_element_type=jnp.float32)
    d_first_ln, g_gain2 = ln_back(d_normed)
    d_first = cotangent.astype(jnp.float32) + d_first_ln
    d_first_b = d_first.astype(jnp.bfloat16)
    g_out = jnp.einsum("pk,pc->kc", mixed_b, d_first_b, preferred_element_type=jnp.float32)
    blended_gradient = jnp.einsum(
        "pc,kc->pk", d_first_b, w_out, preferred_element_type=jnp.float32
    ).reshape(point_count, heads, -1)
    slice_portion_gradient = jnp.einsum(
        "skn,ske->kne", slice_weight_rows, blended_gradient, precision=HIGH_INDEX
    )
    weight_blend_gradient = jnp.einsum(
        "ikl,krl->ikr", blended_gradient, slice_output, precision=HIGH_INDEX
    )
    return (
        d_first,
        weight_blend_gradient,
        slice_portion_gradient,
        g_gain2,
        g_up,
        g_bup,
        g_down,
        g_out,
    )


def back_front(
    normed_b,
    ln_back,
    weight_back,
    slice_weight_rows,
    feature_head_rows,
    d_first,
    weight_blend_gradient,
    numerator_gradient,
    denominator_gradient,
    w_x,
    w_fx,
):
    point_count = slice_weight_rows.shape[0]
    weight_gradient = (
        weight_blend_gradient
        + jnp.einsum("exz,iez->iex", numerator_gradient, feature_head_rows, precision=HIGH_INDEX)
        + denominator_gradient[None, :, :]
    )
    feature_gradient = jnp.einsum(
        "iwe,web->iwb", slice_weight_rows, numerator_gradient, precision=HIGH_INDEX
    ).reshape(point_count, -1)
    d_mid, g_slice, g_base, g_ada = weight_back(weight_gradient)
    d_mid_b = d_mid.astype(jnp.bfloat16)
    d_feat_b = feature_gradient.astype(jnp.bfloat16)
    g_x = jnp.einsum("pc,pk->ck", normed_b, d_mid_b, preferred_element_type=jnp.float32)
    g_fx = jnp.einsum("pc,pk->ck", normed_b, d_feat_b, preferred_element_type=jnp.float32)
    d_normed = jnp.einsum("pk,ck->pc", d_mid_b, w_x, preferred_element_type=jnp.float32)
    d_normed = d_normed + jnp.einsum(
        "pk,ck->pc", d_feat_b, w_fx, preferred_element_type=jnp.float32
    )
    d_points_ln, g_gain1 = ln_back(d_normed)
    grad_points = (d_first + d_points_ln).astype(jnp.bfloat16)
    return (grad_points, g_gain1, g_x, g_fx, g_slice, g_base, g_ada)


def per_device(
    points,
    cotangent,
    ln1_gain,
    w_x,
    w_fx,
    w_slice,
    temp_base,
    ada_vec,
    query_matrix,
    key_matrix,
    value_matrix,
    w_out,
    ln2_gain,
    w_up,
    b_up,
    w_down,
):
    normed_b, ln_back, weight_back, slice_weight_rows, feature_head_rows, numer_part, denom_part = (
        front(points, ln1_gain, w_x, w_fx, w_slice, temp_base, ada_vec)
    )
    numerator_total, denom = lax.psum((numer_part, denom_part), "pts")
    slice_output, token_back = jax.vjp(
        tokens_out, numerator_total, denom, query_matrix, key_matrix, value_matrix
    )
    d_first, weight_blend_gradient, slice_portion_gradient, g_gain2, g_up, g_bup, g_down, g_out = (
        back_top(
            points, cotangent, slice_weight_rows, slice_output, ln2_gain, w_out, w_up, b_up, w_down
        )
    )
    d_slice_out = lax.psum(slice_portion_gradient, "pts")
    numerator_gradient, denominator_gradient, g_q, g_k, g_v = token_back(d_slice_out)
    grad_points, g_gain1, g_x, g_fx, g_slice, g_base, g_ada = back_front(
        normed_b,
        ln_back,
        weight_back,
        slice_weight_rows,
        feature_head_rows,
        d_first,
        weight_blend_gradient,
        numerator_gradient,
        denominator_gradient,
        w_x,
        w_fx,
    )
    g_gain1, g_x, g_fx, g_slice, g_base, g_ada, g_gain2, g_up, g_bup, g_down, g_out = lax.psum(
        (g_gain1, g_x, g_fx, g_slice, g_base, g_ada, g_gain2, g_up, g_bup, g_down, g_out), "pts"
    )
    return (
        grad_points,
        g_gain1,
        g_x,
        g_fx,
        g_slice,
        g_base,
        g_ada,
        g_q,
        g_k,
        g_v,
        g_out,
        g_gain2,
        g_up,
        g_bup,
        g_down,
    )


def solution(mesh):
    placed = (
        P("pts", None),
        P("pts", None),
        P(),
        P(),
        P(),
        P(),
        P(),
        P(),
        P(),
        P(),
        P(),
        P(),
        P(),
        P(),
        P(),
        P(),
    )
    return jax.shard_map(
        per_device,
        mesh=mesh,
        in_specs=placed,
        out_specs=(
            P("pts", None),
            P(),
            P(),
            P(),
            P(),
            P(),
            P(),
            P(),
            P(),
            P(),
            P(),
            P(),
            P(),
            P(),
            P(),
        ),
        check_vma=False,
    )
```

profile of v0, /device:TPU:1, one launch (start us, length us, event | category | flops | bytes accessed | tf_op | source)
XLA Modules:
  0.0 836.4 jit_solution(8329313017826848114)
XLA Ops:
  7.3 1.3 copy.32
  8.9 1.4 fusion.58
  10.8 8.2 fusion.45
  19.0 2.9 copy.41
  22.6 2.2 fusion.62
  26.8 2.6 fusion.69
  30.2 82.0 %psum.99 = f32[8,64]{1,0:T(8,128)S(1)} all-reduce(f32[8,64]{1,0:T(8,128)S(1)} %get-tuple-element.51), channel_id=1, replica_groups=mesh['pts'=256] {'pts'}, use_global_device_ids=true, to_apply=%region_5.0 | all-reduce | flops 512 | bytes 4096 | tf_op jit(solution)/shard_map/psum | solution.py:164
  112.8 2.0 copy.31
  114.8 159.4 %all-reduce.6.cloned.1.call-done = f32[8,64,32]{1,2,0:T(8,128)} async-done(((f32[8,64,32]{1,2,0:T(8,128)}), f32[8,64,32]{1,2,0:T(8,128)}) %all-reduce.6.cloned.1.call-update) | async-done | bytes 65552 | tf_op jit(solution)/shard_map/psum | solution.py:164
  274.3 1.2 fusion.35
  275.5 1.3 fusion.38
  277.4 1.3 fusion.32
  279.1 1.1 convolution_convert_fusion.1
  281.0 0.8 fusion.53
  282.0 2.6 fusion.7
  284.6 4.1 fusion.68
  288.7 1.8 fusion.20
  290.5 1.5 multiply_reduce_fusion.2
  293.2 1.1 fusion.72
  294.6 1.0 copy-done.3
  295.6 2.6 fusion.71
  298.3 4.4 fusion.70
  303.0 1.3 multiply_divide_fusion.3
  304.3 237.2 %all-reduce.8.cloned.1.call-done = f32[8,64,32]{1,2,0:T(8,128)} async-done(((f32[8,64,32]{1,2,0:T(8,128)}), f32[8,64,32]{1,2,0:T(8,128)}) %all-reduce.8.cloned.1.call-update) | async-done | bytes 65552 | tf_op jit(solution)/shard_map/psum | solution.py:173
  541.5 1.6 multiply_reduce_fusion.5
  543.1 1.4 fusion.51
  544.5 1.6 fusion.52
  547.6 1.2 convolution_convert_fusion
  549.0 2.5 multiply_reduce_fusion.1
  551.5 0.9 multiply_reduce_fusion
  552.6 1.5 fusion.12
  554.1 1.1 fusion.56
  555.6 1.1 fusion.54
  556.7 1.4 fusion.19
  559.3 2.3 add_convert_fusion
  561.6 2.1 copy.40
  563.7 2.2 convolution_bitcast_fusion.4
  566.0 3.7 convolution_bitcast_fusion.3
  569.8 77.3 %all-reduce = (f32[256]{0:T(256)}, f32[32,64]{1,0:T(8,128)}, f32[8]{0:T(128)}, f32[32]{0:T(128)}, f32[256]{0:T(256)}, /*index=5*/f32[1024]{0:T(1024)}) all-reduce(f32[256]{0:T(256)S(1)} %get-tuple-element.32, f32[32,64]{1,0:T(8,128)S(1)} %convolution_bitcast_fusion.3, ...), channel_id=1, replica_groups=mesh['pts'=256] {'pts'}, use_global_device_ids=true, to_apply=%region_19.0 | all-reduce | flops 3624 | bytes 28992 | tf_op jit(solution)/shard_map/psum | solution.py:188
  647.1 0.9 convolution_bitcast_fusion.1
  647.9 0.9 convolution_bitcast_fusion.2
  648.8 0.9 convolution_bitcast_fusion
  649.7 171.4 %all-reduce.10.cloned.1.call-done = (f32[256,256]{1,0:T(8,128)}, f32[256,256]{1,0:T(8,128)}, f32[256,256]{1,0:T(8,128)}, f32[256,1024]{1,0:T(8,128)}, f32[1024,256]{1,0:T(8,128)}) async-done(((f32[256,256]{1,0:T(8,128)}, f32[256,256]{1,0:T(8,128)}, f32[256,256]{1,0:T(8,128)}, f32[256,1024]{1,0:T(8,128)}, f32[1024,256]{1,0:T(8,128)}), (f32[256,256]{1,0:T(8,128)}, f32[256,256]{1,0:T(8,128)}, ...) | async-done | bytes 2883600 | tf_op jit(solution)/shard_map/psum | solution.py:188
  821.1 1.8 copy.62
  822.9 1.7 copy.63
  824.5 1.7 copy.64
  826.2 2.3 copy.65
  828.5 1.0 copy.66
  (169 shorter events, 11.5 us)
Async XLA Ops:
  7.2 273.7 %copy-start = (bf16[256,1024]{1,0:T(8,128)(2,1)S(1)}, bf16[256,1024]{1,0:T(8,128)(2,1)}, u32[]{:S(2)}) copy-start(bf16[256,1024]{1,0:T(8,128)(2,1)} %param.29) | copy-start | bytes 1572868
  7.2 3.1 copy-start.18
  7.2 267.0 %all-reduce.6.cloned.1.call-start = ((), (), s32[]{:S(2)}) async-start(), calls=%async_computation | async-start | bytes 262144 | tf_op jit(solution)/shard_map/psum | solution.py:164
  10.7 11.8 %copy-start.4 = (f32[1024,256]{0,1:T(8,128)}, f32[1024,256]{0,1:T(8,128)S(1)}, u32[]{:S(2)}) copy-start(f32[1024,256]{0,1:T(8,128)S(1)} %fusion.60) | copy-start | bytes 3145732
  19.0 2.9 copy-start.57
  19.0 3.6 copy-start.63
  22.5 2.3 copy-start.21
  24.8 4.7 copy-start.24
  26.8 247.5 %copy-start.52 = (f32[32,32]{1,0:T(8,128)S(1)}, f32[32,32]{1,0:T(8,128)}, u32[]{:S(2)}) copy-start(f32[32,32]{1,0:T(8,128)} %param.25) | copy-start | bytes 12292
  26.8 248.7 %copy-start.54 = (f32[32,32]{1,0:T(8,128)S(1)}, f32[32,32]{1,0:T(8,128)}, u32[]{:S(2)}) copy-start(f32[32,32]{1,0:T(8,128)} %param.24) | copy-start | bytes 12292
  29.5 512.0 %all-reduce.8.cloned.1.call-start = ((), (), s32[]{:S(2)}) async-start(), calls=%async_computation.1 | async-start | bytes 262144 | tf_op jit(solution)/shard_map/psum | solution.py:173
  112.8 167.5 %copy-start.45 = (f32[8,64]{1,0:T(8,128)}, f32[8,64]{1,0:T(8,128)S(1)}, u32[]{:S(2)}) copy-start(f32[8,64]{1,0:T(8,128)S(1)} %get-tuple-element.56) | copy-start | bytes 6148
  275.5 3.2 copy-start.40
  277.4 3.2 copy-start.49
  277.4 2.9 copy-start.17
  282.0 2.6 copy-start.62
  292.3 2.2 copy-start.1
  302.7 518.4 %all-reduce.10.cloned.1.call-start = ((), (), s32[]{:S(2)}) async-start(), calls=%async_computation.2 | async-start | bytes 5767168 | tf_op jit(solution)/shard_map/psum | solution.py:188
  541.4 4.7 copy-start.32
  541.4 4.7 copy-start.50
  541.4 5.3 copy-start.51
  541.4 5.6 copy-start.53
  543.1 4.2 copy-start.35
  543.1 4.2 copy-start.48
  543.1 4.2 copy-start.55
  543.1 4.5 copy-start.46
  544.5 4.3 copy-start.37
  544.5 4.4 copy-start.12
  546.2 2.7 copy-start.29
  546.8 4.7 copy-start.33
  546.8 2.1 copy-start.7
  546.8 2.1 copy-start.10
  546.8 2.1 copy-start.22
  546.8 2.1 copy-start.42
  548.9 6.7 copy-start.13
  548.9 2.5 copy-start.25
  549.0 2.5 copy-start.28
  552.6 2.6 copy-start.19
  559.3 6.6 copy-start.23
  561.6 4.3 copy-start.5
  565.9 3.8 copy-start.56
  565.9 3.8 copy-start.59
  565.9 81.1 %copy-start.30 = (f32[8,64,32]{1,2,0:T(8,128)S(1)}, f32[8,64,32]{1,2,0:T(8,128)}, u32[]{:S(2)}) copy-start(f32[8,64,32]{1,2,0:T(8,128)} %copy-done.29) | copy-start | bytes 196612
  566.0 81.1 %copy-start.36 = (f32[8,64,32]{1,2,0:T(8,128)S(1)}, f32[8,64,32]{1,2,0:T(8,128)}, u32[]{:S(2)}) copy-start(f32[8,64,32]{1,2,0:T(8,128)} %all-reduce.6.cloned.1.call-done) | copy-start | bytes 196612
  566.0 81.1 %copy-start.47 = (f32[8,64]{1,0:T(8,128)S(1)}, f32[8,64]{1,0:T(8,128)}, u32[]{:S(2)}) copy-start(f32[8,64]{1,0:T(8,128)} %copy-done.45) | copy-start | bytes 6148
  566.0 82.0 %copy-start.38 = (f32[8,64,32]{1,2,0:T(8,128)S(1)}, f32[8,64,32]{1,2,0:T(8,128)}, u32[]{:S(2)}) copy-start(f32[8,64,32]{1,2,0:T(8,128)} %copy-done.37) | copy-start | bytes 196612
  566.0 82.8 %copy-start.34 = (f32[8,64,32]{1,2,0:T(8,128)S(1)}, f32[8,64,32]{1,2,0:T(8,128)}, u32[]{:S(2)}) copy-start(f32[8,64,32]{1,2,0:T(8,128)} %copy-done.33) | copy-start | bytes 196612
  821.1 7.4 copy-start.14
  (21 other events, 28.3 us)
Sparse Core Ops, SparseCore 0:
  29.6 244.6 all-reduce.5
  302.9 238.5 all-reduce.7
  558.7 262.3 all-reduce.9
where the time goes:
time: 844 us; the launch traced here: 836 us
  waiting for transfers between devices  568 us (67%)
  blocking collectives  159 us (19%)
  matrix products  63.8 us (8%)
  local copies, waits for them, and re-layouts  21.3 us (3%)
  between operations  15.2 us (2%)
    psum x1, waiting for transfers between devices, per_device(): d_slice_out = lax.psum(slice_portion_gradient, 'pts')  237 us
    psum x1, waiting for transfers between devices, per_device(): lax.psum((g_gain1, g_x, g_fx, g_slice, g_base, g_ada, g_gain2, g_up, g_bu...  171 us
    psum x1, waiting for transfers between devices, per_device(): numerator_total, denom = lax.psum((numer_part, denom_part), 'pts')  159 us
    psum x1, blocking collectives, per_device(): numerator_total, denom = lax.psum((numer_part, denom_part), 'pts')  82 us
    psum x1, blocking collectives, per_device(): lax.psum((g_gain1, g_x, g_fx, g_slice, g_base, g_ada, g_gain2, g_up, g_bu...  77.3 us
    unnamed x140, local copies, waits for them, and re-layouts  18.5 us
  transfers between devices with their start and end apart: 3, of which 3 were waited for; matrix products, arithmetic and copies ran while one was open for 2% of the time, Pallas kernels for 0%

commit v1 on v0

v1 whole, which is shorter than its diff:
```python
import jax
import jax.numpy as jnp
from jax import lax
from jax.experimental import pallas as pl
from jax.experimental.pallas import tpu as pltpu
from jax.sharding import PartitionSpec as P

MESH = pl.DeviceIdType.MESH
F32 = jnp.float32
BF16 = jnp.bfloat16
C = 256
HEADS = 8
HEAD_DIM = 32
SLICES = 64
HIDDEN = 1024
LANES = HEADS * SLICES
N = 1024
TILE = 256
EPS = 1e-5
GELU_A = 0.7978845608028654
GELU_B = 0.044715

UP, DOWN, OUT = 0, 1024, 2048
WIDE = 2304
GX, GFX, REST = 0, 256, 512
TAIL = 640


def nn(a, b):
    return lax.dot_general(a, b, (((1,), (0,)), ((), ())), preferred_element_type=F32)


def nt(a, b):
    return lax.dot_general(a, b, (((1,), (1,)), ((), ())), preferred_element_type=F32)


def tn(a, b):
    return lax.dot_general(a, b, (((0,), (0,)), ((), ())), preferred_element_type=F32)


def split(x):
    hi = x.astype(BF16)
    return hi, (x - hi.astype(F32)).astype(BF16)


def exact(dot, a, b):
    ah, al = split(a)
    bh, bl = split(b)
    return dot(ah, bh) + (dot(al, bh) + dot(ah, bl))


def remote(src, dst, send_sem, recv_sem, device):
    return pltpu.make_async_remote_copy(
        src_ref=src,
        dst_ref=dst,
        send_sem=send_sem,
        recv_sem=recv_sem,
        device_id=(device,),
        device_id_type=MESH,
    )


FAR_ZC = (8, 9, 7, 10, 6, 11, 5, 12, 4, 13, 3, 14, 2, 15, 1)
FAR_XY = (10, 9, 11, 6, 14, 8, 2, 5, 7, 13, 15, 1, 3, 4, 12)
FAR_Z = (4, 3, 5, 2, 6, 1, 7)


class Place:
    def __init__(self):
        me = lax.axis_index("pts")
        self.m, self.q = lax.rem(me, 16), lax.div(me, 16)
        self.core, self.z = lax.rem(self.m, 2), lax.div(self.m, 2)

    def zc(self, d):
        return lax.rem(self.m + d, 16)

    def xy(self, d):
        return lax.rem(self.q + d, 16)

    def zc_device(self, d):
        return self.q * 16 + self.zc(d)

    def xy_device(self, d):
        return self.xy(d) * 16 + self.m

    def z_device(self, d):
        return self.q * 16 + lax.rem(self.z + d, 8) * 2 + self.core

    def other_core(self):
        return self.q * 16 + self.z * 2 + (1 - self.core)


def greet(at):
    bar = pltpu.get_barrier_semaphore()
    for d in range(1, 16):
        pl.semaphore_signal(bar, inc=1, device_id=(at.zc_device(d),), device_id_type=MESH)
        pl.semaphore_signal(bar, inc=1, device_id=(at.xy_device(d),), device_id_type=MESH)


def greeted():
    pl.semaphore_wait(pltpu.get_barrier_semaphore(), 30)


class SmallSum:
    def __init__(self, at, x, got, plane, total, sems):
        self.at, self.x, self.got, self.plane, self.total, self.sems = at, x, got, plane, total, sems
        self.sent = []

    def _start(self, copies):
        for c in copies:
            c.start()
        self.phase = copies
        self.sent += copies

    def scatter(self):
        at, s = self.at, self.sems
        self._start(
            [remote(self.x.at[at.zc(d)], self.got.at[d], s.at[0, d], s.at[1, d], at.zc_device(d)) for d in FAR_ZC]
        )

    def middle(self):
        at, s = self.at, self.sems
        for c in self.phase:
            c.wait_recv()
        part = self.x[at.m]
        for d in range(1, 16):
            part = part + self.got[d]
        self.plane[at.q] = part
        mine = self.plane.at[at.q]
        self._start([remote(mine, mine, s.at[2, d], s.at[3, d], at.xy_device(d)) for d in FAR_XY])

    def gather(self):
        at, s = self.at, self.sems
        for c in self.phase:
            c.wait_recv()
        part = self.plane[0]
        for i in range(1, 16):
            part = part + self.plane[i]
        self.total[at.m] = part
        mine = self.total.at[at.m]
        self._start([remote(mine, mine, s.at[4, d], s.at[5, d], at.zc_device(d)) for d in FAR_ZC])

    def finish(self):
        for c in self.phase:
            c.wait_recv()
        for c in self.sent:
            c.wait_send()


class WideSum:
    def __init__(self, at, x, pair, got, column, total, sems):
        self.at, self.x, self.pair, self.got, self.column = at, x, pair, got, column
        self.total, self.sems = total, sems
        self.sent = []

    def _start(self, copies):
        for c in copies:
            c.start()
        self.phase = copies
        self.sent += copies

    def _arrive(self):
        for c in self.phase:
            c.wait_recv()

    def scatter_pair(self):
        at, s = self.at, self.sems
        there = pl.ds((1 - at.core) * 16, 16)
        self._start([remote(self.x.at[there], self.pair, s.at[0, 0], s.at[1, 0], at.other_core())])

    def scatter(self):
        at, s = self.at, self.sems
        self._arrive()
        base = at.core * 16

        def add(i, _):
            self.x[base + i] += self.pair[i]
            return 0

        lax.fori_loop(0, 16, add, 0)
        self._start(
            [
                remote(self.x.at[base + at.xy(d)], self.got.at[d], s.at[2, d], s.at[3, d], at.xy_device(d))
                for d in FAR_XY
            ]
        )

    def middle(self):
        at, s = self.at, self.sems
        self._arrive()
        mine = self.x[at.core * 16 + at.q]
        for d in range(1, 16):
            mine = mine + self.got[d]
        self.column[at.z] = mine
        here = self.column.at[at.z]
        self._start([remote(here, here, s.at[4, d], s.at[5, d], at.z_device(d)) for d in FAR_Z])

    def gather(self):
        at, s = self.at, self.sems
        self._arrive()
        mine = self.column[0]
        for i in range(1, 8):
            mine = mine + self.column[i]
        slot = at.core * 16 + at.q
        self.total[slot] = mine
        here = self.total.at[slot]
        self._start([remote(here, here, s.at[6, d], s.at[7, d], at.xy_device(d)) for d in FAR_XY])

    def gather_pair(self):
        at, s = self.at, self.sems
        self._arrive()
        here = self.total.at[pl.ds(at.core * 16, 16)]
        self._start([remote(here, here, s.at[8, 0], s.at[9, 0], at.other_core())])

    def finish(self):
        self._arrive()
        for c in self.sent:
            c.wait_send()


def iota(shape, axis):
    return lax.broadcasted_iota(jnp.int32, shape, axis)


def head_mask(rows, per_row, columns, per_column):
    return iota((rows, columns), 0) // per_row == iota((rows, columns), 1) // per_column


def column_of(row):
    k = row.shape[1]
    eye = iota((k, k), 0) == iota((k, k), 1)
    return jnp.sum(jnp.where(eye, jnp.broadcast_to(row, (k, k)), 0.0), axis=1, keepdims=True)


def spread_heads(x):
    return jnp.where(head_mask(C, HEAD_DIM, LANES, SLICES), jnp.concatenate([x] * HEADS, axis=0), 0.0)


def fold_heads(x):
    x = jnp.where(head_mask(C, HEAD_DIM, LANES, SLICES), x, 0.0)
    return sum(x[h * HEAD_DIM : (h + 1) * HEAD_DIM] for h in range(HEADS))


def layer_norm(x):
    centered = x - jnp.mean(x, axis=-1, keepdims=True)
    inv = lax.rsqrt(jnp.mean(centered * centered, axis=-1, keepdims=True) + EPS)
    return centered * inv, inv


def layer_norm_back(d, hat, inv):
    a = jnp.mean(d, axis=-1, keepdims=True)
    b = jnp.mean(d * hat, axis=-1, keepdims=True)
    return inv * (d - a - hat * b)


def head_sums(x, ones):
    hi, lo = split(x)
    return jnp.concatenate(
        [nn(hi[:, k : k + 256], ones) + nn(lo[:, k : k + 256], ones) for k in (0, 256)], axis=1
    )


def kernel(
    points, cot, gain1, w_x, w_fx, w_slice, base, ada, wq, wk, wv, w_out, gain2, w_up, b_up, w_down,
    o_points, o_gx, o_gfx, o_gq, o_gk, o_gv, o_gout, o_gup, o_gdown, o_rest,
    nb, hat1, inv1, mid, feat, weight, weight_b, logits, rate, slope,
    hat2, inv2, n2b, act_b, dpre_b, dact, mixed_b, dfirst, dfirst_b, dmixed_b, dweight, dmid_b, dfeat_b, dlog_b, dtilt_b,
    ba_hi, ba_lo, ones, numer, so_b, so_l, dn_b, dn_l, denom_acc, bup_acc, gain2_acc, gain1_acc, base_acc, ada_acc, attn,
    s1_x, s1_got, s1_plane, s1_total, s2_x, s2_got, s2_plane, s2_total,
    wide_x, wide_pair, wide_got, wide_column, wide_total,
    tail_x, tail_pair, tail_got, tail_column, tail_total,
    s1_sems, s2_sems, wide_sems, tail_sems,
):
    at = Place()
    greet(at)
    first_sum = SmallSum(at, s1_x, s1_got, s1_plane, s1_total, s1_sems)
    second_sum = SmallSum(at, s2_x, s2_got, s2_plane, s2_total, s2_sems)
    wide = WideSum(at, wide_x, wide_pair, wide_got, wide_column, wide_total, wide_sems)
    tail = WideSum(at, tail_x, tail_pair, tail_got, tail_column, tail_total, tail_sems)

    ws2 = jnp.concatenate([w_slice[...]] * 2, axis=1)
    hi, lo = split(spread_heads(jnp.concatenate([ws2] * 4, axis=1)))
    ba_hi[:, :LANES], ba_lo[:, :LANES] = hi, lo
    hi, lo = split(spread_heads(jnp.broadcast_to(column_of(ada[...]), (HEAD_DIM, LANES))))
    ba_hi[:, LANES:], ba_lo[:, LANES:] = hi, lo
    ones[...] = jnp.where(head_mask(256, SLICES, 256, SLICES), 1.0, 0.0).astype(BF16)
    base_row = jnp.sum(
        jnp.where(
            iota((HEADS, LANES), 0) == iota((HEADS, LANES), 1) // SLICES,
            jnp.broadcast_to(column_of(base[...]), (HEADS, LANES)),
            0.0,
        ),
        axis=0,
        keepdims=True,
    )
    inv_base = 1.0 / base_row

    numer[...] = jnp.zeros_like(numer)
    denom_acc[...] = jnp.zeros_like(denom_acc)

    def front(i, _):
        rows = pl.ds(pl.multiple_of(i * TILE, TILE), TILE)
        hat, inv = layer_norm(points[rows].astype(F32))
        hat1[rows] = hat
        inv1[rows] = inv
        normed = (hat * gain1[...]).astype(BF16)
        nb[rows] = normed
        md = nn(normed, w_x[...])
        ft = nn(normed, w_fx[...])
        mh, ml = split(md)
        mid[rows] = mh
        lt = nn(mh, ba_hi[...]) + (nn(ml, ba_hi[...]) + nn(mh, ba_lo[...]))
        th = jnp.tanh(lt[:, LANES:])
        rt = jnp.exp(-0.5 * th) * inv_base
        rate[rows] = rt
        slope[rows] = -0.5 * (1.0 - th * th)
        lg = lt[:, :LANES] * rt
        logits[rows] = lg
        raised = jnp.exp(lg)
        w = raised / head_sums(raised, ones[...])
        weight[rows] = w
        denom_acc[...] += jnp.sum(w, axis=0, keepdims=True)
        wh, wl = split(w)
        weight_b[rows] = wh
        fh, fl = split(ft)
        feat[rows] = fh
        numer[...] += tn(fh, wh) + (tn(fl, wh) + tn(fh, wl))
        return 0

    lax.fori_loop(0, N // TILE, front, 0)

    part = fold_heads(numer[...])
    for i in range(4):
        for j in range(4):
            s1_x[i * 4 + j, :8, :] = part[8 * i : 8 * i + 8, 128 * j : 128 * j + 128]
            s1_x[i * 4 + j, 8:, :] = jnp.broadcast_to(denom_acc[:, 128 * j : 128 * j + 128], (8, 128))
    greeted()
    first_sum.scatter()

    def early(i, _):
        rows = pl.ds(pl.multiple_of(i * TILE, TILE), TILE)
        dact[rows] = nt(cot[rows], w_down[...])
        return 0

    lax.fori_loop(0, N // TILE, early, 0)
    first_sum.middle()
    first_sum.gather()
    first_sum.finish()

    numer_t = jnp.concatenate(
        [jnp.concatenate([s1_total[i * 4 + j, :8, :] for j in range(4)], axis=1) for i in range(4)], axis=0
    )
    denom = jnp.concatenate([s1_total[j, 8:9, :] for j in range(4)], axis=1) + EPS
    tok = numer_t / denom
    q_t = exact(tn, wq[...], tok)
    k_t = exact(tn, wk[...], tok)
    v_t = exact(tn, wv[...], tok)
    pair_mask = head_mask(128, SLICES, 128, SLICES)
    scale = HEAD_DIM ** (-0.5)
    outs = []
    for p in range(4):
        c = slice(128 * p, 128 * p + 128)
        e = jnp.where(pair_mask, jnp.exp(exact(tn, q_t[:, c], k_t[:, c]) * scale), 0.0)
        a = e / jnp.sum(e, axis=1, keepdims=True)
        attn[p] = a
        outs.append(exact(nt, v_t[:, c], a))
    so_b[...], so_l[...] = split(spread_heads(jnp.concatenate(outs, axis=1)))

    numer[...] = jnp.zeros_like(numer)
    bup_acc[...] = jnp.zeros_like(bup_acc)
    gain2_acc[...] = jnp.zeros_like(gain2_acc)

    def top(i, _):
        rows = pl.ds(pl.multiple_of(i * TILE, TILE), TILE)
        mb = (nt(weight_b[rows], so_b[...]) + nt(weight_b[rows], so_l[...])).astype(BF16)
        mixed_b[rows] = mb
        first = points[rows].astype(F32) + nn(mb, w_out[...])
        hat, inv = layer_norm(first)
        normed = (hat * gain2[...]).astype(BF16)
        n2b[rows] = normed
        for k in range(0, HIDDEN, 256):
            x = nn(normed, w_up[:, k : k + 256]) + b_up[:, k : k + 256]
            xx = x * x
            t = jnp.tanh(GELU_A * x * (1.0 + GELU_B * xx))
            half = 0.5 * (1.0 + t)
            act_b[rows, k : k + 256] = (x * half).astype(BF16)
            grad = half + (0.5 * GELU_A) * x * (1.0 - t * t) * (1.0 + (3.0 * GELU_B) * xx)
            d = grad * dact[rows, k : k + 256]
            bup_acc[:, k : k + 256] += jnp.sum(d, axis=0, keepdims=True)
            dpre_b[rows, k : k + 256] = d.astype(BF16)
        dn = nt(dpre_b[rows, :], w_up[...])
        gain2_acc[...] += jnp.sum(dn * hat, axis=0, keepdims=True)
        df = cot[rows].astype(F32) + layer_norm_back(dn * gain2[...], hat, inv)
        dfirst[rows] = df
        dfb = df.astype(BF16)
        dfirst_b[rows] = dfb
        dm = nt(dfb, w_out[...])
        dmh, dml = split(dm)
        dmixed_b[rows] = dmh
        wh = weight_b[rows]
        numer[...] += tn(dmh, wh) + tn(dml, wh)
        return 0

    lax.fori_loop(0, N // TILE, top, 0)

    part = fold_heads(numer[...])
    for i in range(4):
        for j in range(4):
            s2_x[i * 4 + j] = part[8 * i : 8 * i + 8, 128 * j : 128 * j + 128]
    second_sum.scatter()

    for k in range(0, HIDDEN, 256):
        wide_x[:, :, UP + k : UP + k + 256] = tn(n2b[...], dpre_b[:, k : k + 256]).reshape(32, 8, 256)
    wide_x[:, :, OUT : OUT + 256] = tn(mixed_b[...], dfirst_b[...]).reshape(32, 8, 256)
    second_sum.middle()
    for k in range(0, HIDDEN, 256):
        g = tn(act_b[:, k : k + 256], cot[...]).reshape(8, 4, 8, 256)
        for j in range(4):
            wide_x[k // 32 : k // 32 + 8, :, DOWN + 256 * j : DOWN + 256 * j + 256] = g[:, j]
    wide.scatter_pair()

    def later(i, _):
        rows = pl.ds(pl.multiple_of(i * TILE, TILE), TILE)
        dweight[rows] = nn(dmixed_b[rows], so_b[...]) + nn(dmixed_b[rows], so_l[...])
        return 0

    second_sum.gather()
    lax.fori_loop(0, N // TILE, later, 0)
    second_sum.finish()

    dso = jnp.concatenate(
        [jnp.concatenate([s2_total[i * 4 + j] for j in range(4)], axis=1) for i in range(4)], axis=0
    )
    dq, dk, dv = [], [], []
    for p in range(4):
        c = slice(128 * p, 128 * p + 128)
        a = attn[p]
        dv.append(exact(nn, dso[:, c], a))
        da = exact(tn, dso[:, c], v_t[:, c])
        ds = a * (da - jnp.sum(a * da, axis=1, keepdims=True)) * scale
        dq.append(exact(nt, k_t[:, c], ds))
        dk.append(exact(nn, q_t[:, c], ds))
    dq, dk, dv = (jnp.concatenate(v, axis=1) for v in (dq, dk, dv))
    o_gq[...] = exact(nt, tok, dq)
    o_gk[...] = exact(nt, tok, dk)
    o_gv[...] = exact(nt, tok, dv)
    dtok = exact(nn, wq[...], dq) + exact(nn, wk[...], dk) + exact(nn, wv[...], dv)
    dnumer = dtok / denom
    ddenom = -jnp.sum(dnumer * tok, axis=0, keepdims=True)
    dn_b[...], dn_l[...] = split(spread_heads(dnumer))

    gain1_acc[...] = jnp.zeros_like(gain1_acc)
    base_acc[...] = jnp.zeros_like(base_acc)
    numer[...] = jnp.zeros_like(numer)
    ada_acc[...] = jnp.zeros_like(ada_acc)

    def lower(i, _):
        rows = pl.ds(pl.multiple_of(i * TILE, TILE), TILE)
        w = weight[rows]
        dw = dweight[rows] + (nn(feat[rows], dn_b[...]) + nn(feat[rows], dn_l[...])) + ddenom
        dl = w * (dw - head_sums(w * dw, ones[...]))
        g = dl * logits[rows]
        base_acc[...] += jnp.sum(g, axis=0, keepdims=True)
        dlb = (dl * rate[rows]).astype(BF16)
        gb = (g * slope[rows]).astype(BF16)
        dlog_b[rows] = dlb
        dtilt_b[rows] = gb
        dm = nt(dlb, ba_hi[:, :LANES]) + nt(gb, ba_hi[:, LANES:])
        dmb = dm.astype(BF16)
        dmid_b[rows] = dmb
        dfb = (nt(weight_b[rows], dn_b[...]) + nt(weight_b[rows], dn_l[...])).astype(BF16)
        dfeat_b[rows] = dfb
        mh = mid[rows]
        numer[...] += tn(mh, dlb)
        ada_acc[...] += tn(mh, gb)
        dn = nt(dmb, w_x[...]) + nt(dfb, w_fx[...])
        hat = hat1[rows]
        gain1_acc[...] += jnp.sum(dn * hat, axis=0, keepdims=True)
        o_points[rows] = (dfirst[rows] + layer_norm_back(dn * gain1[...], hat, inv1[rows])).astype(BF16)
        return 0

    wide.scatter()
    lax.fori_loop(0, N // TILE, lower, 0)
    wide.middle()
    tail_x[:, :, GX : GX + 256] = tn(nb[...], dmid_b[...]).reshape(32, 8, 256)
    tail_x[:, :, GFX : GFX + 256] = tn(nb[...], dfeat_b[...]).reshape(32, 8, 256)
    gs = fold_heads(numer[...])
    ga = fold_heads(ada_acc[...])
    gs = (gs[:, :128] + gs[:, 128:256]) + (gs[:, 256:384] + gs[:, 384:])
    ga = (ga[:, :128] + ga[:, 128:256]) + (ga[:, 256:384] + ga[:, 384:])
    rest = (REST, REST + 128)
    tail_x[:, :, REST : REST + 128] = jnp.zeros((32, 8, 128), F32)
    tail_x[0:4, :, REST : REST + 128] = gs.reshape(4, 8, 128)
    tail_x[4:8, :, REST : REST + 128] = ga.reshape(4, 8, 128)
    for i in range(8):
        tail_x[8, i : i + 1, rest[0] : rest[1]] = bup_acc[:, 128 * i : 128 * i + 128]
    for i in range(4):
        tail_x[9, i : i + 1, rest[0] : rest[1]] = base_acc[:, 128 * i : 128 * i + 128]
    for i in range(2):
        tail_x[10, i : i + 1, rest[0] : rest[1]] = gain1_acc[:, 128 * i : 128 * i + 128]
        tail_x[10, i + 2 : i + 3, rest[0] : rest[1]] = gain2_acc[:, 128 * i : 128 * i + 128]
    tail.scatter_pair()
    tail.scatter()
    wide.gather()
    tail.middle()
    tail.gather()
    wide.gather_pair()
    tail.gather_pair()
    wide.finish()
    tail.finish()
    o_gup[...] = wide_total[:, :, UP : UP + 1024]
    for j in range(4):
        o_gdown[:, j] = wide_total[:, :, DOWN + 256 * j : DOWN + 256 * j + 256]
    o_gout[...] = wide_total[:, :, OUT : OUT + 256]
    o_gx[...] = tail_total[:, :, GX : GX + 256]
    o_gfx[...] = tail_total[:, :, GFX : GFX + 256]

    o_rest[...] = jnp.zeros_like(o_rest)
    gs = tail_total[0:4, :, rest[0] : rest[1]].reshape(32, 128)
    o_rest[0:32, :] = gs + pltpu.roll(gs, 64, 1)
    ga = tail_total[4:8, :, rest[0] : rest[1]].reshape(32, 128)
    ga = jnp.sum(ga, axis=1, keepdims=True)
    o_rest[32:33, 0:32] = jnp.sum(
        jnp.where(iota((32, 32), 0) == iota((32, 32), 1), jnp.broadcast_to(ga, (32, 32)), 0.0), axis=0, keepdims=True
    )
    gb = jnp.concatenate([tail_total[9, i : i + 1, rest[0] : rest[1]] for i in range(4)], axis=1)
    gb = gb * (-inv_base)
    pick = iota((HEADS, LANES), 0) == iota((HEADS, LANES), 1) // SLICES
    gb = jnp.sum(jnp.where(pick, jnp.broadcast_to(gb, (HEADS, LANES)), 0.0), axis=1, keepdims=True)
    o_rest[33:34, 0:8] = jnp.sum(
        jnp.where(iota((8, 8), 0) == iota((8, 8), 1), jnp.broadcast_to(gb, (8, 8)), 0.0), axis=0, keepdims=True
    )
    o_rest[34:38, :] = tail_total[10, 0:4, rest[0] : rest[1]]
    o_rest[40:48, :] = tail_total[8, :, rest[0] : rest[1]]


def per_device(*args):
    (points, cot, gain1, w_x, w_fx, w_slice, base, ada, wq, wk, wv, w_out, gain2, w_up, b_up, w_down) = args
    row = lambda v: v.reshape(1, -1)
    ins = (
        points, cot, row(gain1), w_x, w_fx, w_slice, row(base), row(ada), wq, wk, wv, w_out, row(gain2), w_up,
        row(b_up), w_down,
    )
    spec = pl.BlockSpec(memory_space=pltpu.VMEM)
    outs = [
        ((N, C), BF16),
        ((32, 8, 256), F32),
        ((32, 8, 256), F32),
        ((32, 32), F32),
        ((32, 32), F32),
        ((32, 32), F32),
        ((32, 8, 256), F32),
        ((32, 8, 1024), F32),
        ((32, 4, 8, 256), F32),
        ((48, 128), F32),
    ]
    held = [
        ((N, C), BF16), ((N, C), F32), ((N, 1), F32), ((N, C), BF16), ((N, C), BF16), ((N, LANES), F32),
        ((N, LANES), BF16), ((N, LANES), F32), ((N, LANES), F32), ((N, LANES), F32),
        ((8, C), F32), ((8, 1), F32), ((N, C), BF16), ((N, HIDDEN), BF16), ((N, HIDDEN), BF16), ((N, HIDDEN), F32),
        ((N, C), BF16), ((N, C), F32), ((N, C), BF16), ((N, C), BF16), ((N, LANES), F32), ((N, C), BF16),
        ((N, C), BF16), ((N, LANES), BF16), ((N, LANES), BF16),
        ((C, 2 * LANES), BF16), ((C, 2 * LANES), BF16), ((256, 256), BF16), ((C, LANES), F32), ((C, LANES), BF16), ((C, LANES), BF16),
        ((C, LANES), BF16), ((C, LANES), BF16), ((1, LANES), F32), ((1, HIDDEN), F32), ((1, C), F32), ((1, C), F32), ((1, LANES), F32),
        ((C, LANES), F32), ((4, 128, 128), F32),
        *(((16, 16, 128), F32),) * 4, *(((16, 8, 128), F32),) * 4,
        ((32, 8, WIDE), F32), ((16, 8, WIDE), F32), ((16, 8, WIDE), F32), ((8, 8, WIDE), F32), ((32, 8, WIDE), F32),
        ((32, 8, TAIL), F32), ((16, 8, TAIL), F32), ((16, 8, TAIL), F32), ((8, 8, TAIL), F32), ((32, 8, TAIL), F32),
    ]
    sems = [pltpu.SemaphoreType.DMA((k, 16)) for k in (6, 6, 10, 10)]
    got = pl.pallas_call(
        kernel,
        out_shape=[jax.ShapeDtypeStruct(s, d) for s, d in outs],
        in_specs=[spec] * len(ins),
        out_specs=[spec] * len(outs),
        scratch_shapes=[pltpu.VMEM(s, d) for s, d in held] + sems,
        compiler_params=pltpu.CompilerParams(
            collective_id=1, has_side_effects=True, vmem_limit_bytes=60 << 20
        ),
    )(*ins)
    g_points, g_x, g_fx, g_q, g_k, g_v, g_out, g_up, g_down, rest = got
    return (
        g_points,
        rest[34:36].reshape(C),
        g_x.reshape(C, C),
        g_fx.reshape(C, C),
        rest[0:32, 0:SLICES],
        rest[33, 0:HEADS],
        rest[32, 0:HEAD_DIM],
        g_q,
        g_k,
        g_v,
        g_out.reshape(C, C),
        rest[36:38].reshape(C),
        g_up.reshape(C, HIDDEN),
        rest[40:48].reshape(HIDDEN),
        g_down.reshape(HIDDEN, C),
    )


def solution(mesh):
    rows, whole = P("pts", None), P()
    return jax.shard_map(
        per_device,
        mesh=mesh,
        in_specs=(rows, rows) + (whole,) * 14,
        out_specs=(rows,) + (whole,) * 14,
        check_vma=False,
    )
```

time: 844 us -> 130 us (0.15)
  waiting for transfers between devices: 568 us -> 0 us
  blocking collectives: 159 us -> 0 us
  Pallas kernels: 0 us -> 116 us
  matrix products: 63.8 us -> 0 us
  between operations: 15.2 us -> 0.69 us
  local copies, waits for them, and re-layouts: 21.3 us -> 12.2 us
    psum x3 -> x0, waiting for transfers between devices: 568 us -> none  [the longest x1 237 us: per_device(): d_slice_out = lax.psum(slice_portion_gradient, 'pts')]
    psum x2 -> x0, blocking collectives: 159 us -> none  [the longest x1 82 us: per_device(): numerator_total, denom = lax.psum((numer_part, denom_part), 'pts')]
    pallas_call x0 -> x1, Pallas kernels: none -> 116 us  [per_device(): pl.pallas_call(kernel, out_shape=[jax.ShapeDtypeStruct(s, d) for s, d in...]
    dot_general x40 -> x0, matrix products: 63.8 us -> none  [the longest x2 10.4 us: slice_weights(): jnp.einsum('phd,d->ph', split, ada_vec, precision=HIGH_INDEX)]
    unnamed x140 -> x27, local copies, waits for them, and re-layouts: 18.5 us -> 9.42 us
  transfers between devices with their start and end apart: 3 -> 0, of which waited for: 3 -> 0; matrix products, arithmetic and copies ran while one was open for 2% -> 0% of each run, Pallas kernels for 0% -> 0%
where the time goes in v1:
time: 130 us; the launch traced here: 129 us
  Pallas kernels  116 us (89%)
  local copies, waits for them, and re-layouts  12.2 us (9%)
    pallas_call x1, Pallas kernels, per_device(): pl.pallas_call(kernel, out_shape=[jax.ShapeDtypeStruct(s, d) for s, d in...  116 us
    unnamed x27, local copies, waits for them, and re-layouts  9.42 us

profile of v1, /device:TPU:1, one launch (start us, length us, event | category | flops | bytes accessed | tf_op | source)
XLA Modules:
  0.0 129.4 jit_solution(3070394562813734676)
XLA Ops:
  0.7 116.5 %shard_map.271 = (bf16[1024,256]{1,0:T(8,128)(2,1)}, f32[32,8,256]{2,1,0:T(8,128)}, f32[32,8,256]{2,1,0:T(8,128)}, f32[32,32]{1,0:T(8,128)}, f32[32,32]{1,0:T(8,...) custom-call(bf16[1024,256]{1,0:T(8,128)(2,1)} %points.1, ...), custom_call_target="tpu_custom_call" | custom-call | tf_op jit(solution)/shard_map/pallas_call | solution.py:571
  117.1 0.0 copy-start.5
  117.1 0.7 copy-done.5
  117.9 0.5 slice_bitcast_fusion.3
  118.4 0.5 slice_bitcast_fusion.4
  118.9 0.6 slice_bitcast_fusion.1
  119.5 0.6 slice_bitcast_fusion
  120.1 0.6 slice.19
  120.7 0.0 copy-start.4
  120.7 0.0 copy-start.3
  120.7 0.0 copy-start.8
  120.7 0.0 copy-start.2
  120.7 1.9 %copy.40 = bf16[1024,256]{1,0:T(8,128)(2,1)} copy(bf16[1024,256]{1,0:T(8,128)(2,1)} %get-tuple-element.52) | data formatting | bytes 1048576
  122.6 0.0 copy-done.4
  122.6 0.0 copy-start.1
  122.6 0.7 copy.41
  123.3 0.0 copy-done.3
  123.3 0.7 copy.42
  124.0 0.0 copy-done.8
  124.0 0.0 copy-start.7
  124.0 0.6 copy.43
  124.6 0.1 copy-done.7
  124.8 0.0 copy-start.6
  124.8 0.6 copy.44
  125.4 0.1 copy-done.6
  125.5 0.6 copy.45
  126.1 0.0 copy-done.2
  126.1 0.7 copy.46
  126.8 0.0 copy-done.1
  126.8 0.0 copy-start
  126.8 1.0 copy.47
  127.8 0.6 copy-done
  128.4 1.0 copy.48
Async XLA Ops:
  117.1 0.7 copy-start.5
  120.7 2.0 %copy-start.4 = (f32[32,8,256]{2,1,0:T(8,128)S(1)}, f32[32,8,256]{2,1,0:T(8,128)}, u32[]{:S(2)}) copy-start(f32[32,8,256]{2,1,0:T(8,128)} %get-tuple-element.27) | copy-start | bytes 786436
  120.7 2.7 %copy-start.3 = (f32[32,8,256]{2,1,0:T(8,128)S(1)}, f32[32,8,256]{2,1,0:T(8,128)}, u32[]{:S(2)}) copy-start(f32[32,8,256]{2,1,0:T(8,128)} %get-tuple-element.28) | copy-start | bytes 786436
  120.7 3.4 %copy-start.8 = (f32[32,32]{1,0:T(8,128)S(1)}, f32[32,32]{1,0:T(8,128)}, u32[]{:S(2)}) copy-start(f32[32,32]{1,0:T(8,128)} %get-tuple-element.59) | copy-start | bytes 12292
  120.7 5.4 %copy-start.2 = (f32[32,8,256]{2,1,0:T(8,128)S(1)}, f32[32,8,256]{2,1,0:T(8,128)}, u32[]{:S(2)}) copy-start(f32[32,8,256]{2,1,0:T(8,128)} %get-tuple-element.32) | copy-start | bytes 786436
  122.6 4.2 %copy-start.1 = (f32[32,8,1024]{2,1,0:T(8,128)S(1)}, f32[32,8,1024]{2,1,0:T(8,128)}, u32[]{:S(2)}) copy-start(f32[32,8,1024]{2,1,0:T(8,128)} %get-tuple-element.33) | copy-start | bytes 3145732
  124.0 0.7 copy-start.7
  124.8 0.7 copy-start.6
  126.8 1.6 %copy-start = (f32[32,4,8,256]{3,2,1,0:T(8,128)S(1)}, f32[32,4,8,256]{3,2,1,0:T(8,128)}, u32[]{:S(2)}) copy-start(f32[32,4,8,256]{3,2,1,0:T(8,128)} %get-tuple-element.34) | copy-start | bytes 3145732

commit v2 on v1

--- a/solution.py
+++ b/solution.py
@@ -20,8 +20,8 @@
 GELU_A = 0.7978845608028654
 GELU_B = 0.044715
 
-UP, DOWN, OUT = 0, 1024, 2048
-WIDE = 2304
+UP, DOWN_A, WIDE_A = 0, 1024, 1536
+DOWN_B, OUT, WIDE_B = 0, 512, 768
 GX, GFX, REST = 0, 256, 512
 TAIL = 640
 
@@ -148,10 +148,17 @@
 
 
 class WideSum:
-    def __init__(self, at, x, pair, got, column, total, sems):
+    def __init__(self, at, z_first, x, pair, got, column, total, sems):
         self.at, self.x, self.pair, self.got, self.column = at, x, pair, got, column
         self.total, self.sems = total, sems
+        plane = (FAR_XY, at.q, at.xy, at.xy_device)
+        line = (FAR_Z, at.z, lambda d: lax.rem(at.z + d, 8), at.z_device)
+        self.first, self.second = (line, plane) if z_first else (plane, line)
+        self.per = got.shape[1]
         self.sent = []
+
+    def _slabs(self, index):
+        return pl.ds(self.at.core * 16 + index * self.per, self.per)
 
     def _start(self, copies):
         for c in copies:
@@ -169,42 +176,45 @@
         self._start([remote(self.x.at[there], self.pair, s.at[0, 0], s.at[1, 0], at.other_core())])
 
     def scatter(self):
-        at, s = self.at, self.sems
+        s = self.sems
         self._arrive()
-        base = at.core * 16
+        base = self.at.core * 16
 
         def add(i, _):
             self.x[base + i] += self.pair[i]
             return 0
 
         lax.fori_loop(0, 16, add, 0)
+        far, _, index, device = self.first
         self._start(
             [
-                remote(self.x.at[base + at.xy(d)], self.got.at[d], s.at[2, d], s.at[3, d], at.xy_device(d))
-                for d in FAR_XY
+                remote(self.x.at[self._slabs(index(d))], self.got.at[d], s.at[2, d], s.at[3, d], device(d))
+                for d in far
             ]
         )
 
     def middle(self):
-        at, s = self.at, self.sems
+        s = self.sems
         self._arrive()
-        mine = self.x[at.core * 16 + at.q]
-        for d in range(1, 16):
+        mine = self.x[self._slabs(self.first[1])]
+        for d in range(1, self.got.shape[0]):
             mine = mine + self.got[d]
-        self.column[at.z] = mine
-        here = self.column.at[at.z]
-        self._start([remote(here, here, s.at[4, d], s.at[5, d], at.z_device(d)) for d in FAR_Z])
+        far, own, _, device = self.second
+        self.column[own] = mine
+        here = self.column.at[own]
+        self._start([remote(here, here, s.at[4, d], s.at[5, d], device(d)) for d in far])
 
     def gather(self):
-        at, s = self.at, self.sems
+        s = self.sems
         self._arrive()
         mine = self.column[0]
-        for i in range(1, 8):
+        for i in range(1, self.column.shape[0]):
             mine = mine + self.column[i]
-        slot = at.core * 16 + at.q
-        self.total[slot] = mine
-        here = self.total.at[slot]
-        self._start([remote(here, here, s.at[6, d], s.at[7, d], at.xy_device(d)) for d in FAR_XY])
+        far, own, _, device = self.first
+        slabs = self._slabs(own)
+        self.total[slabs] = mine
+        here = self.total.at[slabs]
+        self._start([remote(here, here, s.at[6, d], s.at[7, d], device(d)) for d in far])
 
     def gather_pair(self):
         at, s = self.at, self.sems
@@ -232,6 +242,12 @@
     return jnp.sum(jnp.where(eye, jnp.broadcast_to(row, (k, k)), 0.0), axis=1, keepdims=True)
 
 
+def row_of(column):
+    k = column.shape[0]
+    eye = iota((k, k), 0) == iota((k, k), 1)
+    return jnp.sum(jnp.where(eye, jnp.broadcast_to(column, (k, k)), 0.0), axis=0, keepdims=True)
+
+
 def spread_heads(x):
     return jnp.where(head_mask(C, HEAD_DIM, LANES, SLICES), jnp.concatenate([x] * HEADS, axis=0), 0.0)
 
@@ -262,21 +278,23 @@
 
 def kernel(
     points, cot, gain1, w_x, w_fx, w_slice, base, ada, wq, wk, wv, w_out, gain2, w_up, b_up, w_down,
-    o_points, o_gx, o_gfx, o_gq, o_gk, o_gv, o_gout, o_gup, o_gdown, o_rest,
+    o_points, o_ggain1, o_gx, o_gfx, o_gslice, o_gbase, o_gada, o_gq, o_gk, o_gv, o_gout, o_ggain2, o_gup, o_gbup, o_gdown,
     nb, hat1, inv1, mid, feat, weight, weight_b, logits, rate, slope,
     hat2, inv2, n2b, act_b, dpre_b, dact, mixed_b, dfirst, dfirst_b, dmixed_b, dweight, dmid_b, dfeat_b, dlog_b, dtilt_b,
     ba_hi, ba_lo, ones, numer, so_b, so_l, dn_b, dn_l, denom_acc, bup_acc, gain2_acc, gain1_acc, base_acc, ada_acc, attn,
     s1_x, s1_got, s1_plane, s1_total, s2_x, s2_got, s2_plane, s2_total,
-    wide_x, wide_pair, wide_got, wide_column, wide_total,
+    a_x, a_pair, a_got, a_column, a_total,
+    b_x, b_pair, b_got, b_column, b_total,
     tail_x, tail_pair, tail_got, tail_column, tail_total,
-    s1_sems, s2_sems, wide_sems, tail_sems,
+    s1_sems, s2_sems, a_sems, b_sems, tail_sems, out_sems, points_out,
 ):
     at = Place()
     greet(at)
     first_sum = SmallSum(at, s1_x, s1_got, s1_plane, s1_total, s1_sems)
     second_sum = SmallSum(at, s2_x, s2_got, s2_plane, s2_total, s2_sems)
-    wide = WideSum(at, wide_x, wide_pair, wide_got, wide_column, wide_total, wide_sems)
-    tail = WideSum(at, tail_x, tail_pair, tail_got, tail_column, tail_total, tail_sems)
+    wide_a = WideSum(at, False, a_x, a_pair, a_got, a_column, a_total, a_sems)
+    wide_b = WideSum(at, True, b_x, b_pair, b_got, b_column, b_total, b_sems)
+    tail = WideSum(at, False, tail_x, tail_pair, tail_got, tail_column, tail_total, tail_sems)
 
     ws2 = jnp.concatenate([w_slice[...]] * 2, axis=1)
     hi, lo = split(spread_heads(jnp.concatenate([ws2] * 4, axis=1)))
@@ -410,14 +428,16 @@
     second_sum.scatter()
 
     for k in range(0, HIDDEN, 256):
-        wide_x[:, :, UP + k : UP + k + 256] = tn(n2b[...], dpre_b[:, k : k + 256]).reshape(32, 8, 256)
-    wide_x[:, :, OUT : OUT + 256] = tn(mixed_b[...], dfirst_b[...]).reshape(32, 8, 256)
+        a_x[:, :, UP + k : UP + k + 256] = tn(n2b[...], dpre_b[:, k : k + 256]).reshape(32, 8, 256)
+    b_x[:, :, OUT : OUT + 256] = tn(mixed_b[...], dfirst_b[...]).reshape(32, 8, 256)
     second_sum.middle()
     for k in range(0, HIDDEN, 256):
         g = tn(act_b[:, k : k + 256], cot[...]).reshape(8, 4, 8, 256)
-        for j in range(4):
-            wide_x[k // 32 : k // 32 + 8, :, DOWN + 256 * j : DOWN + 256 * j + 256] = g[:, j]
-    wide.scatter_pair()
+        for j in range(2):
+            a_x[k // 32 : k // 32 + 8, :, DOWN_A + 256 * j : DOWN_A + 256 * j + 256] = g[:, j]
+            b_x[k // 32 : k // 32 + 8, :, DOWN_B + 256 * j : DOWN_B + 256 * j + 256] = g[:, j + 2]
+    wide_a.scatter_pair()
+    wide_b.scatter_pair()
 
     def later(i, _):
         rows = pl.ds(pl.multiple_of(i * TILE, TILE), TILE)
@@ -425,8 +445,10 @@
         return 0
 
     second_sum.gather()
+    wide_a.scatter()
     lax.fori_loop(0, N // TILE, later, 0)
     second_sum.finish()
+    wide_b.scatter()
 
     dso = jnp.concatenate(
         [jnp.concatenate([s2_total[i * 4 + j] for j in range(4)], axis=1) for i in range(4)], axis=0
@@ -476,12 +498,14 @@
         dn = nt(dmb, w_x[...]) + nt(dfb, w_fx[...])
         hat = hat1[rows]
         gain1_acc[...] += jnp.sum(dn * hat, axis=0, keepdims=True)
-        o_points[rows] = (dfirst[rows] + layer_norm_back(dn * gain1[...], hat, inv1[rows])).astype(BF16)
+        points_out[rows] = (dfirst[rows] + layer_norm_back(dn * gain1[...], hat, inv1[rows])).astype(BF16)
         return 0
 
-    wide.scatter()
     lax.fori_loop(0, N // TILE, lower, 0)
-    wide.middle()
+    leaving = [pltpu.make_async_copy(points_out, o_points, out_sems.at[0])]
+    leaving[0].start()
+    wide_a.middle()
+    wide_b.middle()
     tail_x[:, :, GX : GX + 256] = tn(nb[...], dmid_b[...]).reshape(32, 8, 256)
     tail_x[:, :, GFX : GFX + 256] = tn(nb[...], dfeat_b[...]).reshape(32, 8, 256)
     gs = fold_heads(numer[...])
@@ -501,37 +525,61 @@
         tail_x[10, i + 2 : i + 3, rest[0] : rest[1]] = gain2_acc[:, 128 * i : 128 * i + 128]
     tail.scatter_pair()
     tail.scatter()
-    wide.gather()
+    wide_a.gather()
+    wide_b.gather()
     tail.middle()
     tail.gather()
-    wide.gather_pair()
+    wide_a.gather_pair()
+    wide_b.gather_pair()
     tail.gather_pair()
-    wide.finish()
+    wide_a.finish()
+    wide_b.finish()
     tail.finish()
-    o_gup[...] = wide_total[:, :, UP : UP + 1024]
-    for j in range(4):
-        o_gdown[:, j] = wide_total[:, :, DOWN + 256 * j : DOWN + 256 * j + 256]
-    o_gout[...] = wide_total[:, :, OUT : OUT + 256]
-    o_gx[...] = tail_total[:, :, GX : GX + 256]
-    o_gfx[...] = tail_total[:, :, GFX : GFX + 256]
-
-    o_rest[...] = jnp.zeros_like(o_rest)
+    def leave(src, dst):
+        c = pltpu.make_async_copy(src, dst, out_sems.at[len(leaving)])
+        c.start()
+        leaving.append(c)
+
+    leave(a_total.at[:, :, UP : UP + 1024], o_gup)
+    for j in range(2):
+        leave(a_total.at[:, :, DOWN_A + 256 * j : DOWN_A + 256 * j + 256], o_gdown.at[:, j])
+        leave(b_total.at[:, :, DOWN_B + 256 * j : DOWN_B + 256 * j + 256], o_gdown.at[:, j + 2])
+    leave(b_total.at[:, :, OUT : OUT + 256], o_gout)
+    leave(tail_total.at[:, :, GX : GX + 256], o_gx)
+    leave(tail_total.at[:, :, GFX : GFX + 256], o_gfx)
+
     gs = tail_total[0:4, :, rest[0] : rest[1]].reshape(32, 128)
-    o_rest[0:32, :] = gs + pltpu.roll(gs, 64, 1)
+    o_gslice[...] = (gs + pltpu.roll(gs, SLICES, 1))[:, :SLICES]
     ga = tail_total[4:8, :, rest[0] : rest[1]].reshape(32, 128)
-    ga = jnp.sum(ga, axis=1, keepdims=True)
-    o_rest[32:33, 0:32] = jnp.sum(
-        jnp.where(iota((32, 32), 0) == iota((32, 32), 1), jnp.broadcast_to(ga, (32, 32)), 0.0), axis=0, keepdims=True
-    )
+    o_gada[...] = row_of(jnp.sum(ga, axis=1, keepdims=True))
     gb = jnp.concatenate([tail_total[9, i : i + 1, rest[0] : rest[1]] for i in range(4)], axis=1)
     gb = gb * (-inv_base)
     pick = iota((HEADS, LANES), 0) == iota((HEADS, LANES), 1) // SLICES
     gb = jnp.sum(jnp.where(pick, jnp.broadcast_to(gb, (HEADS, LANES)), 0.0), axis=1, keepdims=True)
-    o_rest[33:34, 0:8] = jnp.sum(
-        jnp.where(iota((8, 8), 0) == iota((8, 8), 1), jnp.broadcast_to(gb, (8, 8)), 0.0), axis=0, keepdims=True
-    )
-    o_rest[34:38, :] = tail_total[10, 0:4, rest[0] : rest[1]]
-    o_rest[40:48, :] = tail_total[8, :, rest[0] : rest[1]]
+    o_gbase[...] = row_of(gb)
+    for i in range(2):
+        o_ggain1[:, 128 * i : 128 * i + 128] = tail_total[10, i : i + 1, rest[0] : rest[1]]
+        o_ggain2[:, 128 * i : 128 * i + 128] = tail_total[10, i + 2 : i + 3, rest[0] : rest[1]]
+    for i in range(8):
+        o_gbup[:, 128 * i : 128 * i + 128] = tail_total[8, i : i + 1, rest[0] : rest[1]]
+    for c in leaving:
+        c.wait()
+
+
+def write_out(*refs):
+    sems = refs[-1]
+    count = (len(refs) - 1) // 2
+    copies = [pltpu.make_async_copy(refs[i], refs[count + i], sems.at[i]) for i in range(count)]
+    for c in copies:
+        c.start()
+    for c in copies:
+        c.wait()
+
+
+def wide_buffers(columns, first, second, per):
+    return [
+        (shape + (8, columns), F32) for shape in ((32,), (16,), (first, per), (second, per), (32,))
+    ]
 
 
 def per_device(*args):
@@ -543,17 +591,11 @@
     )
     spec = pl.BlockSpec(memory_space=pltpu.VMEM)
     outs = [
-        ((N, C), BF16),
-        ((32, 8, 256), F32),
-        ((32, 8, 256), F32),
-        ((32, 32), F32),
-        ((32, 32), F32),
-        ((32, 32), F32),
-        ((32, 8, 256), F32),
-        ((32, 8, 1024), F32),
-        ((32, 4, 8, 256), F32),
-        ((48, 128), F32),
+        ((N, C), BF16), ((1, C), F32), ((32, 8, 256), F32), ((32, 8, 256), F32), ((HEAD_DIM, SLICES), F32),
+        ((1, HEADS), F32), ((1, HEAD_DIM), F32), ((32, 32), F32), ((32, 32), F32), ((32, 32), F32),
+        ((32, 8, 256), F32), ((1, C), F32), ((32, 8, 1024), F32), ((1, HIDDEN), F32), ((32, 4, 8, 256), F32),
     ]
+    large = (0, 2, 3, 10, 12, 14)
     held = [
         ((N, C), BF16), ((N, C), F32), ((N, 1), F32), ((N, C), BF16), ((N, C), BF16), ((N, LANES), F32),
         ((N, LANES), BF16), ((N, LANES), F32), ((N, LANES), F32), ((N, LANES), F32),
@@ -564,38 +606,33 @@
         ((C, LANES), BF16), ((C, LANES), BF16), ((1, LANES), F32), ((1, HIDDEN), F32), ((1, C), F32), ((1, C), F32), ((1, LANES), F32),
         ((C, LANES), F32), ((4, 128, 128), F32),
         *(((16, 16, 128), F32),) * 4, *(((16, 8, 128), F32),) * 4,
-        ((32, 8, WIDE), F32), ((16, 8, WIDE), F32), ((16, 8, WIDE), F32), ((8, 8, WIDE), F32), ((32, 8, WIDE), F32),
-        ((32, 8, TAIL), F32), ((16, 8, TAIL), F32), ((16, 8, TAIL), F32), ((8, 8, TAIL), F32), ((32, 8, TAIL), F32),
+        *wide_buffers(WIDE_A, 16, 8, 1), *wide_buffers(WIDE_B, 8, 16, 2), *wide_buffers(TAIL, 16, 8, 1),
     ]
-    sems = [pltpu.SemaphoreType.DMA((k, 16)) for k in (6, 6, 10, 10)]
+    sems = [pltpu.SemaphoreType.DMA((k, 16)) for k in (6, 6, 10, 10, 10)]
+    sems += [pltpu.SemaphoreType.DMA((9,)), pltpu.VMEM((N, C), BF16)]
+    anywhere = pl.BlockSpec(memory_space=pl.ANY)
     got = pl.pallas_call(
         kernel,
         out_shape=[jax.ShapeDtypeStruct(s, d) for s, d in outs],
         in_specs=[spec] * len(ins),
-        out_specs=[spec] * len(outs),
+        out_specs=[anywhere if i in large else spec for i in range(len(outs))],
         scratch_shapes=[pltpu.VMEM(s, d) for s, d in held] + sems,
         compiler_params=pltpu.CompilerParams(
             collective_id=1, has_side_effects=True, vmem_limit_bytes=60 << 20
         ),
     )(*ins)
-    g_points, g_x, g_fx, g_q, g_k, g_v, g_out, g_up, g_down, rest = got
-    return (
-        g_points,
-        rest[34:36].reshape(C),
-        g_x.reshape(C, C),
-        g_fx.reshape(C, C),
-        rest[0:32, 0:SLICES],
-        rest[33, 0:HEADS],
-        rest[32, 0:HEAD_DIM],
-        g_q,
-        g_k,
-        g_v,
-        g_out.reshape(C, C),
-        rest[36:38].reshape(C),
-        g_up.reshape(C, HIDDEN),
-        rest[40:48].reshape(HIDDEN),
-        g_down.reshape(HIDDEN, C),
-    )
+    got = pl.pallas_call(
+        write_out,
+        out_shape=[jax.ShapeDtypeStruct(s, d) for s, d in outs],
+        in_specs=[spec] * len(outs),
+        out_specs=[anywhere] * len(outs),
+        scratch_shapes=[pltpu.SemaphoreType.DMA((len(outs),))],
+    )(*got)
+    shapes = (
+        (N, C), (C,), (C, C), (C, C), (HEAD_DIM, SLICES), (HEADS,), (HEAD_DIM,), (32, 32), (32, 32), (32, 32), (C, C),
+        (C,), (C, HIDDEN), (HIDDEN,), (HIDDEN, C),
+    )
+    return tuple(g.reshape(s) for g, s in zip(got, shapes))
 
 
 def solution(mesh):

time: 130 us -> 113 us (0.87)
  local copies, waits for them, and re-layouts: 12.2 us -> 0 us
  Pallas kernels: 116 us -> 112 us
    unnamed x27 -> x0, local copies, waits for them, and re-layouts: 9.42 us -> none
    pallas_call x1, Pallas kernels: 116 us -> 108 us  [per_device(): pl.pallas_call(kernel, out_shape=[jax.ShapeDtypeStruct(s, d) for s, d in...]
    pallas_call x0 -> x1, Pallas kernels: none -> 3.98 us  [per_device(): pl.pallas_call(write_out, out_shape=[jax.ShapeDtypeStruct(s, d) for s, d...]
where the time goes in v2:
time: 113 us
  Pallas kernels  112 us (99%)
    pallas_call x1, Pallas kernels, per_device(): pl.pallas_call(kernel, out_shape=[jax.ShapeDtypeStruct(s, d) for s, d in...  108 us
    pallas_call x1, Pallas kernels, per_device(): pl.pallas_call(write_out, out_shape=[jax.ShapeDtypeStruct(s, d) for s, d...  3.98 us

profile of v2, /device:TPU:1, one launch (start us, length us, event | category | flops | bytes accessed | tf_op | source)
XLA Modules:
  0.0 113.1 jit_solution(2947591545508111207)
XLA Ops:
  0.7 108.4 %shard_map.271 = (bf16[1024,256]{1,0:T(8,128)(2,1)}, f32[1,256]{1,0:T(1,128)}, f32[32,8,256]{2,1,0:T(8,128)}, f32[32,8,256]{2,1,0:T(8,128)}, f32[32,64]{1,0:T(8,...) custom-call(bf16[1024,256]{1,0:T(8,128)(2,1)} %points.1, ...), custom_call_target="tpu_custom_call" | custom-call | tf_op jit(solution)/shard_map/pallas_call | solution.py:614
  109.1 4.0 %shard_map.272 = (bf16[1024,256]{1,0:T(8,128)(2,1)}, f32[1,256]{1,0:T(1,128)}, f32[32,8,256]{2,1,0:T(8,128)}, f32[32,8,256]{2,1,0:T(8,128)}, f32[32,64]{1,0:T(8,...) custom-call(bf16[1024,256]{1,0:T(8,128)(2,1)} %get-tuple-element.45., ...), custom_call_target="tpu_custom_call" | custom-call | tf_op jit(solution)/shard_map/pallas_call | solution.py:624

commit v3 on v2

--- a/solution.py
+++ b/solution.py
@@ -15,7 +15,8 @@
 HIDDEN = 1024
 LANES = HEADS * SLICES
 N = 1024
-TILE = 256
+TILE = 1024
+PIECE = 1024
 EPS = 1e-5
 GELU_A = 0.7978845608028654
 GELU_B = 0.044715
@@ -218,9 +219,21 @@
 
     def gather_pair(self):
         at, s = self.at, self.sems
-        self._arrive()
-        here = self.total.at[pl.ds(at.core * 16, 16)]
-        self._start([remote(here, here, s.at[8, 0], s.at[9, 0], at.other_core())])
+        far, own, _, _ = self.first
+        count = len(far) + 1
+
+        def forward(d):
+            here = self.total.at[self._slabs(lax.rem(own + (count - d), count))]
+            c = remote(here, here, s.at[8, d], s.at[9, d], at.other_core())
+            c.start()
+            return c
+
+        passed = [forward(0)]
+        for d, c in reversed(list(zip(far, self.phase))):
+            c.wait_recv()
+            passed.append(forward(d))
+        self.phase = passed
+        self.sent += passed
 
     def finish(self):
         self._arrive()
@@ -286,7 +299,7 @@
     a_x, a_pair, a_got, a_column, a_total,
     b_x, b_pair, b_got, b_column, b_total,
     tail_x, tail_pair, tail_got, tail_column, tail_total,
-    s1_sems, s2_sems, a_sems, b_sems, tail_sems, out_sems, points_out,
+    s1_sems, s2_sems, a_sems, b_sems, tail_sems, out_sems, points_out, cot_t, nb_t, mid_t, wide_tile, half_tile,
 ):
     at = Place()
     greet(at)
@@ -327,14 +340,22 @@
         ft = nn(normed, w_fx[...])
         mh, ml = split(md)
         mid[rows] = mh
-        lt = nn(mh, ba_hi[...]) + (nn(ml, ba_hi[...]) + nn(mh, ba_lo[...]))
-        th = jnp.tanh(lt[:, LANES:])
-        rt = jnp.exp(-0.5 * th) * inv_base
-        rate[rows] = rt
-        slope[rows] = -0.5 * (1.0 - th * th)
-        lg = lt[:, :LANES] * rt
-        logits[rows] = lg
-        raised = jnp.exp(lg)
+        wide_tile[...] = nn(mh, ba_hi[...]) + (nn(ml, ba_hi[...]) + nn(mh, ba_lo[...]))
+
+        def raise_piece(j, _):
+            here = pl.ds(pl.multiple_of(j * PIECE, PIECE), PIECE)
+            there = pl.ds(pl.multiple_of(i * TILE + j * PIECE, PIECE), PIECE)
+            th = jnp.tanh(wide_tile[here, LANES:])
+            rt = jnp.exp(-0.5 * th) * inv_base
+            rate[there] = rt
+            slope[there] = -0.5 * (1.0 - th * th)
+            lg = wide_tile[here, :LANES] * rt
+            logits[there] = lg
+            half_tile[here] = jnp.exp(lg)
+            return 0
+
+        lax.fori_loop(0, TILE // PIECE, raise_piece, 0)
+        raised = half_tile[...]
         w = raised / head_sums(raised, ones[...])
         weight[rows] = w
         denom_acc[...] += jnp.sum(w, axis=0, keepdims=True)
@@ -342,7 +363,8 @@
         weight_b[rows] = wh
         fh, fl = split(ft)
         feat[rows] = fh
-        numer[...] += tn(fh, wh) + (tn(fl, wh) + tn(fh, wl))
+        fht = fh.T
+        numer[...] += nn(fht, wh) + (nn(fl.T, wh) + nn(fht, wl))
         return 0
 
     lax.fori_loop(0, N // TILE, front, 0)
@@ -351,13 +373,16 @@
     for i in range(4):
         for j in range(4):
             s1_x[i * 4 + j, :8, :] = part[8 * i : 8 * i + 8, 128 * j : 128 * j + 128]
-            s1_x[i * 4 + j, 8:, :] = jnp.broadcast_to(denom_acc[:, 128 * j : 128 * j + 128], (8, 128))
+            s1_x[i * 4 + j, 8:, :] = denom_acc[:, 128 * j : 128 * j + 128]
     greeted()
     first_sum.scatter()
 
     def early(i, _):
         rows = pl.ds(pl.multiple_of(i * TILE, TILE), TILE)
         dact[rows] = nt(cot[rows], w_down[...])
+        cot_t[:, rows] = cot[rows].T
+        nb_t[:, rows] = nb[rows].T
+        mid_t[:, rows] = mid[rows].T
         return 0
 
     lax.fori_loop(0, N // TILE, early, 0)
@@ -396,16 +421,25 @@
         hat, inv = layer_norm(first)
         normed = (hat * gain2[...]).astype(BF16)
         n2b[rows] = normed
-        for k in range(0, HIDDEN, 256):
-            x = nn(normed, w_up[:, k : k + 256]) + b_up[:, k : k + 256]
-            xx = x * x
-            t = jnp.tanh(GELU_A * x * (1.0 + GELU_B * xx))
-            half = 0.5 * (1.0 + t)
-            act_b[rows, k : k + 256] = (x * half).astype(BF16)
-            grad = half + (0.5 * GELU_A) * x * (1.0 - t * t) * (1.0 + (3.0 * GELU_B) * xx)
-            d = grad * dact[rows, k : k + 256]
-            bup_acc[:, k : k + 256] += jnp.sum(d, axis=0, keepdims=True)
-            dpre_b[rows, k : k + 256] = d.astype(BF16)
+        wide_tile[...] = nn(normed, w_up[...])
+
+        def gelu_piece(j, _):
+            here = pl.ds(pl.multiple_of(j * PIECE, PIECE), PIECE)
+            there = pl.ds(pl.multiple_of(i * TILE + j * PIECE, PIECE), PIECE)
+            for k in range(0, HIDDEN, 256):
+                lanes = slice(k, k + 256)
+                x = wide_tile[here, lanes] + b_up[:, lanes]
+                xx = x * x
+                t = jnp.tanh(GELU_A * x * (1.0 + GELU_B * xx))
+                half = 0.5 + 0.5 * t
+                act_b[there, lanes] = (x * half).astype(BF16)
+                grad = half + x * (0.5 * GELU_A - (0.5 * GELU_A) * (t * t)) * (1.0 + (3.0 * GELU_B) * xx)
+                d = grad * dact[there, lanes]
+                bup_acc[:, lanes] += jnp.sum(d, axis=0, keepdims=True)
+                dpre_b[there, lanes] = d.astype(BF16)
+            return 0
+
+        lax.fori_loop(0, TILE // PIECE, gelu_piece, 0)
         dn = nt(dpre_b[rows, :], w_up[...])
         gain2_acc[...] += jnp.sum(dn * hat, axis=0, keepdims=True)
         df = cot[rows].astype(F32) + layer_norm_back(dn * gain2[...], hat, inv)
@@ -427,12 +461,13 @@
             s2_x[i * 4 + j] = part[8 * i : 8 * i + 8, 128 * j : 128 * j + 128]
     second_sum.scatter()
 
+    n2b_t = n2b[...].T
     for k in range(0, HIDDEN, 256):
-        a_x[:, :, UP + k : UP + k + 256] = tn(n2b[...], dpre_b[:, k : k + 256]).reshape(32, 8, 256)
+        a_x[:, :, UP + k : UP + k + 256] = nn(n2b_t, dpre_b[:, k : k + 256]).reshape(32, 8, 256)
     b_x[:, :, OUT : OUT + 256] = tn(mixed_b[...], dfirst_b[...]).reshape(32, 8, 256)
     second_sum.middle()
     for k in range(0, HIDDEN, 256):
-        g = tn(act_b[:, k : k + 256], cot[...]).reshape(8, 4, 8, 256)
+        g = nn(cot_t[...], act_b[:, k : k + 256]).T.reshape(8, 4, 8, 256)
         for j in range(2):
             a_x[k // 32 : k // 32 + 8, :, DOWN_A + 256 * j : DOWN_A + 256 * j + 256] = g[:, j]
             b_x[k // 32 : k // 32 + 8, :, DOWN_B + 256 * j : DOWN_B + 256 * j + 256] = g[:, j + 2]
@@ -492,9 +527,9 @@
         dmid_b[rows] = dmb
         dfb = (nt(weight_b[rows], dn_b[...]) + nt(weight_b[rows], dn_l[...])).astype(BF16)
         dfeat_b[rows] = dfb
-        mh = mid[rows]
-        numer[...] += tn(mh, dlb)
-        ada_acc[...] += tn(mh, gb)
+        mt = mid_t[:, rows]
+        numer[...] += nn(mt, dlb)
+        ada_acc[...] += nn(mt, gb)
         dn = nt(dmb, w_x[...]) + nt(dfb, w_fx[...])
         hat = hat1[rows]
         gain1_acc[...] += jnp.sum(dn * hat, axis=0, keepdims=True)
@@ -506,8 +541,8 @@
     leaving[0].start()
     wide_a.middle()
     wide_b.middle()
-    tail_x[:, :, GX : GX + 256] = tn(nb[...], dmid_b[...]).reshape(32, 8, 256)
-    tail_x[:, :, GFX : GFX + 256] = tn(nb[...], dfeat_b[...]).reshape(32, 8, 256)
+    tail_x[:, :, GX : GX + 256] = nn(nb_t[...], dmid_b[...]).reshape(32, 8, 256)
+    tail_x[:, :, GFX : GFX + 256] = nn(nb_t[...], dfeat_b[...]).reshape(32, 8, 256)
     gs = fold_heads(numer[...])
     ga = fold_heads(ada_acc[...])
     gs = (gs[:, :128] + gs[:, 128:256]) + (gs[:, 256:384] + gs[:, 384:])
@@ -567,12 +602,17 @@
 
 
 def write_out(*refs):
+    count = len(refs) // 3
     sems = refs[-1]
-    count = (len(refs) - 1) // 2
-    copies = [pltpu.make_async_copy(refs[i], refs[count + i], sems.at[i]) for i in range(count)]
-    for c in copies:
+    ins, outs, held = refs[:count], refs[count : 2 * count], refs[2 * count : 3 * count]
+    arriving = [pltpu.make_async_copy(ins[i], held[i], sems.at[0, i]) for i in range(count)]
+    leaving = [pltpu.make_async_copy(held[i], outs[i], sems.at[1, i]) for i in range(count)]
+    for c in arriving:
         c.start()
-    for c in copies:
+    for a, c in zip(arriving, leaving):
+        a.wait()
+        c.start()
+    for c in leaving:
         c.wait()
 
 
@@ -605,11 +645,12 @@
         ((C, 2 * LANES), BF16), ((C, 2 * LANES), BF16), ((256, 256), BF16), ((C, LANES), F32), ((C, LANES), BF16), ((C, LANES), BF16),
         ((C, LANES), BF16), ((C, LANES), BF16), ((1, LANES), F32), ((1, HIDDEN), F32), ((1, C), F32), ((1, C), F32), ((1, LANES), F32),
         ((C, LANES), F32), ((4, 128, 128), F32),
-        *(((16, 16, 128), F32),) * 4, *(((16, 8, 128), F32),) * 4,
+        *(((16, 9, 128), F32),) * 4, *(((16, 8, 128), F32),) * 4,
         *wide_buffers(WIDE_A, 16, 8, 1), *wide_buffers(WIDE_B, 8, 16, 2), *wide_buffers(TAIL, 16, 8, 1),
     ]
     sems = [pltpu.SemaphoreType.DMA((k, 16)) for k in (6, 6, 10, 10, 10)]
     sems += [pltpu.SemaphoreType.DMA((9,)), pltpu.VMEM((N, C), BF16)]
+    sems += [pltpu.VMEM((C, N), BF16)] * 3 + [pltpu.VMEM((TILE, HIDDEN), F32), pltpu.VMEM((TILE, LANES), F32)]
     anywhere = pl.BlockSpec(memory_space=pl.ANY)
     got = pl.pallas_call(
         kernel,
@@ -624,9 +665,9 @@
     got = pl.pallas_call(
         write_out,
         out_shape=[jax.ShapeDtypeStruct(s, d) for s, d in outs],
-        in_specs=[spec] * len(outs),
+        in_specs=[anywhere] * len(outs),
         out_specs=[anywhere] * len(outs),
-        scratch_shapes=[pltpu.SemaphoreType.DMA((len(outs),))],
+        scratch_shapes=[pltpu.VMEM(s, d) for s, d in outs] + [pltpu.SemaphoreType.DMA((2, len(outs)))],
     )(*got)
     shapes = (
         (N, C), (C,), (C, C), (C, C), (HEAD_DIM, SLICES), (HEADS,), (HEAD_DIM,), (32, 32), (32, 32), (32, 32), (C, C),

time: 113 us -> 107 us (0.947)
  Pallas kernels: 112 us -> 106 us
    pallas_call x1, Pallas kernels: 108 us -> 103 us  [per_device(): pl.pallas_call(kernel, out_shape=[jax.ShapeDtypeStruct(s, d) for s, d in...]
where the time goes in v3:
time: 107 us
  Pallas kernels  106 us (99%)
    pallas_call x1, Pallas kernels, per_device(): pl.pallas_call(kernel, out_shape=[jax.ShapeDtypeStruct(s, d) for s, d in...  103 us
    pallas_call x1, Pallas kernels, per_device(): pl.pallas_call(write_out, out_shape=[jax.ShapeDtypeStruct(s, d) for s, d...  3.34 us

profile of v3, /device:TPU:1, one launch (start us, length us, event | category | flops | bytes accessed | tf_op | source)
XLA Modules:
  0.0 106.8 jit_solution(12259936543715382903)
XLA Ops:
  0.7 102.6 %shard_map.271 = (bf16[1024,256]{1,0:T(8,128)(2,1)}, f32[1,256]{1,0:T(1,128)}, f32[32,8,256]{2,1,0:T(8,128)}, f32[32,8,256]{2,1,0:T(8,128)}, f32[32,64]{1,0:T(8,...) custom-call(bf16[1024,256]{1,0:T(8,128)(2,1)} %points.1, ...), custom_call_target="tpu_custom_call" | custom-call | tf_op jit(solution)/shard_map/pallas_call | solution.py:655
  103.3 3.3 %shard_map.272 = (bf16[1024,256]{1,0:T(8,128)(2,1)}, f32[1,256]{1,0:T(1,128)}, f32[32,8,256]{2,1,0:T(8,128)}, f32[32,8,256]{2,1,0:T(8,128)}, f32[32,64]{1,0:T(8,...) custom-call(bf16[1024,256]{1,0:T(8,128)(2,1)} %get-tuple-element.45., ...), custom_call_target="tpu_custom_call" | custom-call | tf_op jit(solution)/shard_map/pallas_call | solution.py:665

commit v4 on v3

--- a/solution.py
+++ b/solution.py
@@ -21,10 +21,8 @@
 GELU_A = 0.7978845608028654
 GELU_B = 0.044715
 
-UP, DOWN_A, WIDE_A = 0, 1024, 1536
-DOWN_B, OUT, WIDE_B = 0, 512, 768
-GX, GFX, REST = 0, 256, 512
-TAIL = 640
+GX, GFX, OUT, REST = 0, 256, 512, 768
+TAIL = 896
 
 
 def nn(a, b):
@@ -71,6 +69,7 @@
         me = lax.axis_index("pts")
         self.m, self.q = lax.rem(me, 16), lax.div(me, 16)
         self.core, self.z = lax.rem(self.m, 2), lax.div(self.m, 2)
+        self.x, self.y = lax.div(self.q, 4), lax.rem(self.q, 4)
 
     def zc(self, d):
         return lax.rem(self.m + d, 16)
@@ -83,6 +82,18 @@
 
     def xy_device(self, d):
         return self.xy(d) * 16 + self.m
+
+    def along_x(self, d):
+        return lax.rem(self.x + d, 4)
+
+    def along_y(self, d):
+        return lax.rem(self.y + d, 4)
+
+    def x_device(self, d):
+        return (self.along_x(d) * 4 + self.y) * 16 + self.m
+
+    def y_device(self, d):
+        return (self.x * 4 + self.along_y(d)) * 16 + self.m
 
     def z_device(self, d):
         return self.q * 16 + lax.rem(self.z + d, 8) * 2 + self.core
@@ -241,6 +252,110 @@
             c.wait_send()
 
 
+class DeepSum:
+    def __init__(self, at, y_first, x, pair, got, got2, line, line_got, line_sum, total, sems):
+        self.at, self.x, self.pair, self.got, self.got2 = at, x, pair, got, got2
+        self.line, self.line_got, self.line_sum = line, line_got, line_sum
+        self.total, self.sems = total, sems
+        along_x = (at.x, at.along_x, at.x_device)
+        along_y = (at.y, at.along_y, at.y_device)
+        self.first, self.second = (along_y, along_x) if y_first else (along_x, along_y)
+        self.base = at.core * 16
+        self.slab = self.base + 4 * self.first[0] + self.second[0]
+        self.sent = []
+
+    def _chunk(self, index):
+        return pl.ds(self.base + 4 * index, 4)
+
+    def _start(self, step, moves):
+        s = self.sems
+        copies = [remote(src, dst, s.at[2 * step, d], s.at[2 * step + 1, d], device) for d, src, dst, device in moves]
+        for c in copies:
+            c.start()
+        self.phase = copies
+        self.sent += copies
+
+    def _arrive(self):
+        for c in self.phase:
+            c.wait_recv()
+
+    def scatter_pair(self):
+        there = pl.ds((1 - self.at.core) * 16, 16)
+        self._start(0, [(0, self.x.at[there], self.pair, self.at.other_core())])
+
+    def scatter(self):
+        self._arrive()
+
+        def add(i, _):
+            self.x[self.base + i] += self.pair[i]
+            return 0
+
+        lax.fori_loop(0, 16, add, 0)
+        _, index, device = self.first
+        self._start(1, [(d, self.x.at[self._chunk(index(d))], self.got.at[d], device(d)) for d in (2, 1, 3)])
+
+    def scatter_second(self):
+        self._arrive()
+        own = self.base + 4 * self.first[0]
+
+        def add(i, _):
+            self.x[own + i] += self.got[1, i] + (self.got[2, i] + self.got[3, i])
+            return 0
+
+        lax.fori_loop(0, 4, add, 0)
+        _, index, device = self.second
+        self._start(2, [(d, self.x.at[own + index(d)], self.got2.at[d], device(d)) for d in (2, 1, 3)])
+
+    def scatter_line(self):
+        self._arrive()
+        mine = self.x[self.slab] + self.got2[1] + (self.got2[2] + self.got2[3])
+        for i in range(8):
+            self.line[i] = mine[:, 128 * i : 128 * i + 128]
+        at = self.at
+        self._start(
+            3, [(d, self.line.at[lax.rem(at.z + d, 8)], self.line_got.at[d], at.z_device(d)) for d in FAR_Z]
+        )
+
+    def gather_line(self):
+        self._arrive()
+        at = self.at
+        part = self.line[at.z]
+        for d in range(1, 8):
+            part = part + self.line_got[d]
+        self.line_sum[at.z] = part
+        here = self.line_sum.at[at.z]
+        self._start(4, [(d, here, here, at.z_device(d)) for d in FAR_Z])
+
+    def gather_second(self):
+        self._arrive()
+        self.total[self.slab] = jnp.concatenate([self.line_sum[i] for i in range(8)], axis=1)
+        here = self.total.at[self.slab]
+        _, _, device = self.second
+        self._start(5, [(d, here, here, device(d)) for d in (2, 1, 3)])
+
+    def gather(self):
+        self._arrive()
+        own, _, device = self.first
+        here = self.total.at[self._chunk(own)]
+        self._start(6, [(d, here, here, device(d)) for d in (2, 1, 3)])
+
+    def gather_pair(self):
+        own, _, _ = self.first
+        arriving, passed = self.phase, []
+        for d, c in ((0, None), (1, arriving[1]), (3, arriving[2]), (2, arriving[0])):
+            if c is not None:
+                c.wait_recv()
+            here = self.total.at[self._chunk(lax.rem(own + (4 - d), 4))]
+            self._start(7, [(d, here, here, self.at.other_core())])
+            passed += self.phase
+        self.phase = passed
+
+    def finish(self):
+        self._arrive()
+        for c in self.sent:
+            c.wait_send()
+
+
 def iota(shape, axis):
     return lax.broadcasted_iota(jnp.int32, shape, axis)
 
@@ -296,17 +411,19 @@
     hat2, inv2, n2b, act_b, dpre_b, dact, mixed_b, dfirst, dfirst_b, dmixed_b, dweight, dmid_b, dfeat_b, dlog_b, dtilt_b,
     ba_hi, ba_lo, ones, numer, so_b, so_l, dn_b, dn_l, denom_acc, bup_acc, gain2_acc, gain1_acc, base_acc, ada_acc, attn,
     s1_x, s1_got, s1_plane, s1_total, s2_x, s2_got, s2_plane, s2_total,
-    a_x, a_pair, a_got, a_column, a_total,
-    b_x, b_pair, b_got, b_column, b_total,
+    up_x, up_pair, up_got, up_got2, up_line, up_line_got, up_line_sum, up_total,
+    down_x, down_pair, down_got, down_got2, down_line, down_line_got, down_line_sum, down_total,
     tail_x, tail_pair, tail_got, tail_column, tail_total,
-    s1_sems, s2_sems, a_sems, b_sems, tail_sems, out_sems, points_out, cot_t, nb_t, mid_t, wide_tile, half_tile,
+    s1_sems, s2_sems, up_sems, down_sems, tail_sems, out_sems, points_out, cot_t, nb_t, mid_t, wide_tile, half_tile,
 ):
     at = Place()
     greet(at)
     first_sum = SmallSum(at, s1_x, s1_got, s1_plane, s1_total, s1_sems)
     second_sum = SmallSum(at, s2_x, s2_got, s2_plane, s2_total, s2_sems)
-    wide_a = WideSum(at, False, a_x, a_pair, a_got, a_column, a_total, a_sems)
-    wide_b = WideSum(at, True, b_x, b_pair, b_got, b_column, b_total, b_sems)
+    up = DeepSum(at, False, up_x, up_pair, up_got, up_got2, up_line, up_line_got, up_line_sum, up_total, up_sems)
+    down = DeepSum(
+        at, True, down_x, down_pair, down_got, down_got2, down_line, down_line_got, down_line_sum, down_total, down_sems
+    )
     tail = WideSum(at, False, tail_x, tail_pair, tail_got, tail_column, tail_total, tail_sems)
 
     ws2 = jnp.concatenate([w_slice[...]] * 2, axis=1)
@@ -463,16 +580,14 @@
 
     n2b_t = n2b[...].T
     for k in range(0, HIDDEN, 256):
-        a_x[:, :, UP + k : UP + k + 256] = nn(n2b_t, dpre_b[:, k : k + 256]).reshape(32, 8, 256)
-    b_x[:, :, OUT : OUT + 256] = tn(mixed_b[...], dfirst_b[...]).reshape(32, 8, 256)
+        up_x[:, :, k : k + 256] = nn(n2b_t, dpre_b[:, k : k + 256]).reshape(32, 8, 256)
     second_sum.middle()
     for k in range(0, HIDDEN, 256):
         g = nn(cot_t[...], act_b[:, k : k + 256]).T.reshape(8, 4, 8, 256)
-        for j in range(2):
-            a_x[k // 32 : k // 32 + 8, :, DOWN_A + 256 * j : DOWN_A + 256 * j + 256] = g[:, j]
-            b_x[k // 32 : k // 32 + 8, :, DOWN_B + 256 * j : DOWN_B + 256 * j + 256] = g[:, j + 2]
-    wide_a.scatter_pair()
-    wide_b.scatter_pair()
+        for j in range(4):
+            down_x[k // 32 : k // 32 + 8, :, 256 * j : 256 * j + 256] = g[:, j]
+    up.scatter_pair()
+    down.scatter_pair()
 
     def later(i, _):
         rows = pl.ds(pl.multiple_of(i * TILE, TILE), TILE)
@@ -480,10 +595,11 @@
         return 0
 
     second_sum.gather()
-    wide_a.scatter()
+    up.scatter()
+    down.scatter()
     lax.fori_loop(0, N // TILE, later, 0)
+    tail_x[:, :, OUT : OUT + 256] = tn(mixed_b[...], dfirst_b[...]).reshape(32, 8, 256)
     second_sum.finish()
-    wide_b.scatter()
 
     dso = jnp.concatenate(
         [jnp.concatenate([s2_total[i * 4 + j] for j in range(4)], axis=1) for i in range(4)], axis=0
@@ -536,11 +652,13 @@
         points_out[rows] = (dfirst[rows] + layer_norm_back(dn * gain1[...], hat, inv1[rows])).astype(BF16)
         return 0
 
+    up.scatter_second()
+    down.scatter_second()
     lax.fori_loop(0, N // TILE, lower, 0)
     leaving = [pltpu.make_async_copy(points_out, o_points, out_sems.at[0])]
     leaving[0].start()
-    wide_a.middle()
-    wide_b.middle()
+    up.scatter_line()
+    down.scatter_line()
     tail_x[:, :, GX : GX + 256] = nn(nb_t[...], dmid_b[...]).reshape(32, 8, 256)
     tail_x[:, :, GFX : GFX + 256] = nn(nb_t[...], dfeat_b[...]).reshape(32, 8, 256)
     gs = fold_heads(numer[...])
@@ -558,28 +676,31 @@
     for i in range(2):
         tail_x[10, i : i + 1, rest[0] : rest[1]] = gain1_acc[:, 128 * i : 128 * i + 128]
         tail_x[10, i + 2 : i + 3, rest[0] : rest[1]] = gain2_acc[:, 128 * i : 128 * i + 128]
-    tail.scatter_pair()
-    tail.scatter()
-    wide_a.gather()
-    wide_b.gather()
-    tail.middle()
-    tail.gather()
-    wide_a.gather_pair()
-    wide_b.gather_pair()
-    tail.gather_pair()
-    wide_a.finish()
-    wide_b.finish()
-    tail.finish()
     def leave(src, dst):
         c = pltpu.make_async_copy(src, dst, out_sems.at[len(leaving)])
         c.start()
         leaving.append(c)
 
-    leave(a_total.at[:, :, UP : UP + 1024], o_gup)
-    for j in range(2):
-        leave(a_total.at[:, :, DOWN_A + 256 * j : DOWN_A + 256 * j + 256], o_gdown.at[:, j])
-        leave(b_total.at[:, :, DOWN_B + 256 * j : DOWN_B + 256 * j + 256], o_gdown.at[:, j + 2])
-    leave(b_total.at[:, :, OUT : OUT + 256], o_gout)
+    tail.scatter_pair()
+    up.gather_line()
+    down.gather_line()
+    tail.scatter()
+    up.gather_second()
+    down.gather_second()
+    tail.middle()
+    up.gather()
+    down.gather()
+    tail.gather()
+    up.gather_pair()
+    down.gather_pair()
+    up.finish()
+    down.finish()
+    leave(up_total, o_gup)
+    for j in range(4):
+        leave(down_total.at[:, :, 256 * j : 256 * j + 256], o_gdown.at[:, j])
+    tail.gather_pair()
+    tail.finish()
+    leave(tail_total.at[:, :, OUT : OUT + 256], o_gout)
     leave(tail_total.at[:, :, GX : GX + 256], o_gx)
     leave(tail_total.at[:, :, GFX : GFX + 256], o_gfx)
 
@@ -614,6 +735,11 @@
         c.start()
     for c in leaving:
         c.wait()
+
+
+def deep_buffers():
+    shapes = [(32, 8, 1024), (16, 8, 1024), (4, 4, 8, 1024), (4, 8, 1024), *((8, 8, 128),) * 3, (32, 8, 1024)]
+    return [(shape, F32) for shape in shapes]
 
 
 def wide_buffers(columns, first, second, per):
@@ -646,9 +772,9 @@
         ((C, LANES), BF16), ((C, LANES), BF16), ((1, LANES), F32), ((1, HIDDEN), F32), ((1, C), F32), ((1, C), F32), ((1, LANES), F32),
         ((C, LANES), F32), ((4, 128, 128), F32),
         *(((16, 9, 128), F32),) * 4, *(((16, 8, 128), F32),) * 4,
-        *wide_buffers(WIDE_A, 16, 8, 1), *wide_buffers(WIDE_B, 8, 16, 2), *wide_buffers(TAIL, 16, 8, 1),
+        *deep_buffers(), *deep_buffers(), *wide_buffers(TAIL, 16, 8, 1),
     ]
-    sems = [pltpu.SemaphoreType.DMA((k, 16)) for k in (6, 6, 10, 10, 10)]
+    sems = [pltpu.SemaphoreType.DMA((k, 16)) for k in (6, 6, 16, 16, 10)]
     sems += [pltpu.SemaphoreType.DMA((9,)), pltpu.VMEM((N, C), BF16)]
     sems += [pltpu.VMEM((C, N), BF16)] * 3 + [pltpu.VMEM((TILE, HIDDEN), F32), pltpu.VMEM((TILE, LANES), F32)]
     anywhere = pl.BlockSpec(memory_space=pl.ANY)

time: 107 us -> 97.6 us (0.912)
  Pallas kernels: 106 us -> 96.7 us
    pallas_call x1, Pallas kernels: 103 us -> 93.4 us  [per_device(): pl.pallas_call(kernel, out_shape=[jax.ShapeDtypeStruct(s, d) for s, d in...]
where the time goes in v4:
time: 97.6 us; the launch traced here: 97.5 us
  Pallas kernels  96.7 us (99%)
    pallas_call x1, Pallas kernels, per_device(): pl.pallas_call(kernel, out_shape=[jax.ShapeDtypeStruct(s, d) for s, d in...  93.4 us
    pallas_call x1, Pallas kernels, per_device(): pl.pallas_call(write_out, out_shape=[jax.ShapeDtypeStruct(s, d) for s, d...  3.34 us

profile of v4, /device:TPU:1, one launch (start us, length us, event | category | flops | bytes accessed | tf_op | source)
XLA Modules:
  0.0 97.5 jit_solution(3126689417973113335)
XLA Ops:
  0.7 93.4 %shard_map.271 = (bf16[1024,256]{1,0:T(8,128)(2,1)}, f32[1,256]{1,0:T(1,128)}, f32[32,8,256]{2,1,0:T(8,128)}, f32[32,8,256]{2,1,0:T(8,128)}, f32[32,64]{1,0:T(8,...) custom-call(bf16[1024,256]{1,0:T(8,128)(2,1)} %points.1, ...), custom_call_target="tpu_custom_call" | custom-call | tf_op jit(solution)/shard_map/pallas_call | solution.py:781
  94.0 3.3 %shard_map.272 = (bf16[1024,256]{1,0:T(8,128)(2,1)}, f32[1,256]{1,0:T(1,128)}, f32[32,8,256]{2,1,0:T(8,128)}, f32[32,8,256]{2,1,0:T(8,128)}, f32[32,64]{1,0:T(8,...) custom-call(bf16[1024,256]{1,0:T(8,128)(2,1)} %get-tuple-element.45., ...), custom_call_target="tpu_custom_call" | custom-call | tf_op jit(solution)/shard_map/pallas_call | solution.py:791
